TPU v7x, 512 devices: a whole 4x4x16 slice. The times are simulated.
512 devices in a mesh: depth: 16 (over x, y), tile: 32 (over z, core).
Axes of the slice: x: 4, y: 4, z: 16, core: 2. Of those that a mesh axis runs over, the one named last changes fastest.
Arguments:
- volume: bfloat16 [1024, 512, 1024], P('depth', 'tile'), may hold values from -6 to 6
Outputs:
- image: float32 [4, 512, 1024], P(None, 'tile', 'depth')
All inputs are finite; a program needn't handle non-finite values.
Results may differ from a plain program's by a relative error of at most 0.0003.
Values may be sent and summed in bfloat16 or wider, within the bound.
A program may use at most 64 MiB of HBM per device.

v0:
```python
import jax
import jax.numpy as jnp
from jax import lax
from jax.sharding import PartitionSpec as P

light_x = 1.0 / 3.0
light_y = 2.0 / 3.0
light_z = 2.0 / 3.0


def extended(value, sides, width):
    for axis, dim in sides:
        count, length = (lax.axis_size(axis), value.shape[dim])
        up = [(i, (i + 1) % count) for i in range(count - 1)]
        down = [(j, i) for i, j in up]
        last = lax.slice_in_dim(value, length - width, length, axis=dim)
        leading = lax.slice_in_dim(value, 0, width, axis=dim)
        before = lax.ppermute(last, axis, up)
        after = lax.ppermute(leading, axis, down)
        value = jnp.concatenate([before, value, after], axis=dim)
    return value


def render(slab, step):
    core = slab[2:-2, 2:-2]
    grad_z = (
        slab[:-4, 2:-2] - 8.0 * slab[1:-3, 2:-2] + 8.0 * slab[3:-1, 2:-2] - slab[4:, 2:-2]
    ) / 12.0
    grad_x = (
        slab[2:-2, :-4] - 8.0 * slab[2:-2, 1:-3] + 8.0 * slab[2:-2, 3:-1] - slab[2:-2, 4:]
    ) / 12.0
    sided = jnp.pad(core, ((0, 0), (0, 0), (2, 2)))
    grad_y = (
        sided[:, :, :-4] - 8.0 * sided[:, :, 1:-3] + 8.0 * sided[:, :, 3:-1] - sided[:, :, 4:]
    ) / 12.0
    facing = jnp.abs(light_x * grad_x + light_y * grad_y + light_z * grad_z)
    facing = facing * lax.rsqrt(grad_x * grad_x + grad_y * grad_y + grad_z * grad_z + 1.0)
    shading = 0.15 + 0.85 * facing
    optical = (1.0 + core * core) * step
    coverage = 1.0 - jnp.exp(-optical)
    running = jnp.cumsum(optical, axis=0)
    weight = jnp.exp(-(running - optical)) * coverage * shading
    red = jnp.sum(weight * (1.0 + 0.5 * core), axis=0)
    green = jnp.sum(weight * (1.0 - 0.3 * core + 0.2 * core * core), axis=0)
    blue = jnp.sum(weight * (1.0 + 0.25 * core - 0.1 * core * core), axis=0)
    return (jnp.stack([red, green, blue], 0), jnp.exp(-running[-1]))


def body(volume):
    groups = lax.axis_size("depth")
    step = 1.0 / (volume.shape[0] * groups)
    padded = extended(volume, (("depth", 0), ("tile", 1)), 2)
    color, transmit = render(padded.astype(jnp.float32), step)
    rows_here = color.shape[1]
    cols_all = color.shape[2]
    parts_color, parts_trans = (
        lax.all_to_all(
            color.reshape(3, 1, rows_here, cols_all),
            "depth",
            split_axis=3,
            concat_axis=1,
            tiled=True,
        ),
        lax.all_to_all(
            transmit.reshape(1, 1, rows_here, cols_all),
            "depth",
            split_axis=3,
            concat_axis=1,
            tiled=True,
        ),
    )
    through = jnp.cumprod(parts_trans, axis=1)
    before = jnp.concatenate([jnp.ones_like(through[:, :1]), through[:, :-1]], axis=1)
    final_color = jnp.sum(before * parts_color, axis=1)
    final_trans = through[:, -1]
    return jnp.concatenate([final_color, 1.0 - final_trans], 0)


def solution(mesh):
    return jax.shard_map(
        body,
        mesh=mesh,
        in_specs=(P("depth", "tile", None),),
        out_specs=P(None, "tile", "depth"),
        check_vma=False,
    )
```

profile of v0, /device:TPU:225, one launch (start us, length us, event | category | flops | bytes accessed | tf_op | source)
XLA Modules:
  0.0 118.9 jit_solution(3088952532443656589)
XLA Ops:
  0.0 0.9 fusion.28
  0.9 3.2 %collective-permute-start = (bf16[2,16,1024]{2,1,0:T(8,128)(2,1)S(1)}, bf16[2,16,1024]{2,1,0:T(8,128)(2,1)S(1)}, u32[]{:S(2)}, u32[]{:S(2)}) collective-permute-start(bf16[2,16,1024]{2,1,0:T(8,128)(2,1)S(1)} %get-tuple-element.11), channel_id=1, source_target_pairs={{0,32},{32,64},{64,96},{96,128},{128,160},{160,192},{192,224},{224... | collective-permute-start | bytes 196616 | tf_op jit(solution)/shard_map/ppermute | solution.py:18
  4.1 1.3 %collective-permute-start.1 = (bf16[2,16,1024]{2,1,0:T(8,128)(2,1)S(1)}, bf16[2,16,1024]{2,1,0:T(8,128)(2,1)S(1)}, u32[]{:S(2)}, u32[]{:S(2)}) collective-permute-start(bf16[2,16,1024]{2,1,0:T(8,128)(2,1)S(1)} %get-tuple-element.10), channel_id=1, source_target_pairs={{32,0},{64,32},{96,64},{128,96},{160,128},{192,160},{224,192},{256... | collective-permute-start | bytes 196616 | tf_op jit(solution)/shard_map/ppermute | solution.py:19
  5.4 1.8 %constant_dynamic-update-slice_fusion.1 = bf16[68,16,1024]{2,1,0:T(8,128)(2,1)S(1)} fusion(bf16[68,16,1024]{2,1,0:T(8,128)(2,1)S(1)} %constant_dynamic-update-slice_fusion.2, bf16[64,16,1024]{2,1,0:T(8,128)(2,1)} %param.1), kind=kLoop, calls=%fused_computation.47 | loop fusion | bytes 4194304
  7.2 1.9 %collective-permute-done.1 = bf16[2,16,1024]{2,1,0:T(8,128)(2,1)S(1)} collective-permute-done((bf16[2,16,1024]{2,1,0:T(8,128)(2,1)S(1)}, bf16[2,16,1024]{2,1,0:T(8,128)(2,1)S(1)}, u32[]{:S(2)}, u32[]{:S(2)}) %collective-permute-start.1) | collective-permute-done | bytes 65568 | tf_op jit(solution)/shard_map/ppermute | solution.py:19
  9.1 0.5 fusion.27
  9.6 6.7 %collective-permute-start.2 = (bf16[68,2,1024]{2,1,0:T(2,128)(2,1)S(1)}, bf16[68,2,1024]{2,1,0:T(2,128)(2,1)S(1)}, u32[]{:S(2)}, u32[]{:S(2)}) collective-permute-start(bf16[68,2,1024]{2,1,0:T(2,128)(2,1)S(1)} %get-tuple-element.8), channel_id=1, source_target_pairs={{0,1},{1,2},{2,3},{3,4},{4,5},{5,6},{6,7},{7,8},{8,9},{9,10},{10,1... | collective-permute-start | bytes 835592 | tf_op jit(solution)/shard_map/ppermute | solution.py:18
  16.3 1.9 %collective-permute-start.3 = (bf16[68,2,1024]{2,1,0:T(2,128)(2,1)S(1)}, bf16[68,2,1024]{2,1,0:T(2,128)(2,1)S(1)}, u32[]{:S(2)}, u32[]{:S(2)}) collective-permute-start(bf16[68,2,1024]{2,1,0:T(2,128)(2,1)S(1)} %get-tuple-element.9), channel_id=1, source_target_pairs={{1,0},{2,1},{3,2},{4,3},{5,4},{6,5},{7,6},{8,7},{9,8},{10,9},{11,1... | collective-permute-start | bytes 835592 | tf_op jit(solution)/shard_map/ppermute | solution.py:19
  18.3 1.5 %collective-permute-done.2 = bf16[68,2,1024]{2,1,0:T(2,128)(2,1)S(1)} collective-permute-done((bf16[68,2,1024]{2,1,0:T(2,128)(2,1)S(1)}, bf16[68,2,1024]{2,1,0:T(2,128)(2,1)S(1)}, u32[]{:S(2)}, u32[]{:S(2)}) %collective-permute-start.2) | collective-permute-done | bytes 278560 | tf_op jit(solution)/shard_map/ppermute | solution.py:18
  19.8 5.6 %collective-permute-done.3 = bf16[68,2,1024]{2,1,0:T(2,128)(2,1)S(1)} collective-permute-done((bf16[68,2,1024]{2,1,0:T(2,128)(2,1)S(1)}, bf16[68,2,1024]{2,1,0:T(2,128)(2,1)S(1)}, u32[]{:S(2)}, u32[]{:S(2)}) %collective-permute-start.3) | collective-permute-done | bytes 278560 | tf_op jit(solution)/shard_map/ppermute | solution.py:19
  25.4 1.6 %maximum_convert_fusion = f32[68,20,1024]{2,1,0:T(8,128)S(1)} fusion(bf16[68,2,1024]{2,1,0:T(2,128)(2,1)S(1)} %collective-permute-done.3, bf16[68,16,1024]{2,1,0:T(8,128)(2,1)S(1)} %constant_dynamic-update-slice_fusion, bf16[68,2,1024]{2,1,0:T(2,128)(2,1)S(1)} %collective-permute-done.2), kind=kLoop, calls=%fused_computation.31 | loop fusion | flops 8355840 | bytes 8355840 | tf_op jit(solution)/shard_map/convert_element_type | solution.py:53
  27.1 2.8 %copy-done = f32[68,20,1024]{2,1,0:T(8,128)} copy-done((f32[68,20,1024]{2,1,0:T(8,128)}, f32[68,20,1024]{2,1,0:T(8,128)S(1)}, u32[]{:S(2)}) %copy-start) | copy-done | bytes 5570584
  29.9 2.9 %slice.82 = f32[64,16,1024]{2,1,0:T(8,128)} slice(f32[68,20,1024]{2,1,0:T(8,128)S(1)} %maximum_convert_fusion), slice={[2:66], [2:18], [0:1024]} | slice | bytes 8388608 | tf_op jit(solution)/shard_map/slice | solution.py:25
  32.8 42.3 %multiply_reduce_fusion = (f32[16,1024]{1,0:T(8,128)S(1)}, f32[16,1024]{1,0:T(8,128)S(1)}, f32[16,1024]{1,0:T(8,128)S(1)}, f32[64,16,1024]{2,1,0:T(8,128)}) fusion(f32[68,20,1024]{2,1,0:T(8,128)} %copy-done, f32[64,16,1024]{2,1,0:T(8,128)} %slice.82), kind=kOutput, calls=%fused_computation.27 | output fusion | flops 132071424 | bytes 50528256 | tf_op jit(solution)/shard_map/jit(cumsum)/reduce_window_sum | solution.py:41
  75.1 0.9 fusion.22
  76.0 0.3 copy.14
  76.3 0.5 broadcast.47
  76.8 1.9 %reduce = f32[1024,16]{1,0:T(8,128)S(1)} reduce(f32[1024,1,1,16]{3,2,1,0:T(1,128)S(1)} %bitcast.34, f32[]{:T(128)} %broadcast.47), dimensions={1,2}, to_apply=%bitcast.27.reduce_sub_computation | reduce | bytes 131076
  78.7 0.8 reshape.34
  79.6 8.0 %all-to-all-start = ((f32[16,1,1024]{2,1,0:T(1,128)}), f32[16,1,1024]{2,1,0:T(1,128)S(1)}, u32[]{:S(2)}, u32[]{:S(2)}) async-start(f32[16,1,1024]{2,1,0:T(1,128)} %reshape.34), calls=%async_computation | async-start | bytes 131072 | tf_op jit(solution)/shard_map/all_to_all | solution.py:64
  87.6 2.7 %copy.17 = f32[3,1,16,1024]{2,1,0,3:T(1,128)} copy(f32[3,1,16,1024]{3,2,0,1:T(8,128)S(1)} %maximum_bitcast_fusion) | data formatting | bytes 393216 | tf_op jit(solution)/shard_map/reshape | solution.py:58
  90.3 6.5 %reduce.2 = f32[1024,3,16]{2,1,0:T(4,128)S(1)} reduce(f32[1024,3,1,16]{3,2,1,0:T(1,128)} %bitcast.32, f32[]{:T(128)} %broadcast.47), dimensions={2}, to_apply=%bitcast.29.reduce_sub_computation | reduce | bytes 393220
  96.8 1.9 %reshape.36 = f32[16,1,3072]{2,1,0:T(1,128)} reshape(f32[1024,3,16]{2,1,0:T(4,128)S(1)} %reduce.2) | data formatting | bytes 393216
  98.8 6.6 %all-to-all-start.1 = ((f32[16,1,3072]{2,1,0:T(1,128)}), f32[16,1,3072]{2,1,0:T(1,128)S(1)}, u32[]{:S(2)}, u32[]{:S(2)}) async-start(f32[16,1,3072]{2,1,0:T(1,128)} %reshape.36), calls=%async_computation.1 | async-start | bytes 393216 | tf_op jit(solution)/shard_map/all_to_all | solution.py:57
  105.4 0.8 reduce.1
  106.2 0.9 reshape.35
  107.3 0.6 fusion.19
  108.1 4.2 %all-to-all-done.1 = f32[16,1,3072]{2,1,0:T(1,128)S(1)} async-done(((f32[16,1,3072]{2,1,0:T(1,128)}), f32[16,1,3072]{2,1,0:T(1,128)S(1)}, u32[]{:S(2)}, u32[]{:S(2)}) %all-to-all-start.1) | async-done | bytes 196640 | tf_op jit(solution)/shard_map/all_to_all | solution.py:57
  112.3 1.1 reduce.3
  113.5 2.9 %reshape.37 = f32[1024,3,1,16]{3,2,1,0:T(1,128)S(1)} reshape(f32[16,3072]{1,0:T(8,128)S(1)} %reduce.3) | data formatting | bytes 393216
  116.4 1.7 %copy.18 = f32[3,1,16,1024]{3,2,0,1:T(8,128)S(1)} copy(f32[3,1,16,1024]{2,1,0,3:T(1,128)S(1)} %bitcast.31) | data formatting | bytes 393216 | tf_op jit(solution)/shard_map/all_to_all | solution.py:57
  118.3 0.6 pad_maximum_fusion
  (13 shorter events, 0.5 us)
Async XLA Ops:
  0.9 4.5 %collective-permute-start = (bf16[2,16,1024]{2,1,0:T(8,128)(2,1)S(1)}, bf16[2,16,1024]{2,1,0:T(8,128)(2,1)S(1)}, u32[]{:S(2)}, u32[]{:S(2)}) collective-permute-start(bf16[2,16,1024]{2,1,0:T(8,128)(2,1)S(1)} %get-tuple-element.11), channel_id=1, source_target_pairs={{0,32},{32,64},{64,96},{96,128},{128,160},{160,192},{192,224},{224... | collective-permute-start | bytes 196616 | tf_op jit(solution)/shard_map/ppermute | solution.py:18
  4.1 5.0 %collective-permute-start.1 = (bf16[2,16,1024]{2,1,0:T(8,128)(2,1)S(1)}, bf16[2,16,1024]{2,1,0:T(8,128)(2,1)S(1)}, u32[]{:S(2)}, u32[]{:S(2)}) collective-permute-start(bf16[2,16,1024]{2,1,0:T(8,128)(2,1)S(1)} %get-tuple-element.10), channel_id=1, source_target_pairs={{32,0},{64,32},{96,64},{128,96},{160,128},{192,160},{224,192},{256... | collective-permute-start | bytes 196616 | tf_op jit(solution)/shard_map/ppermute | solution.py:19
  9.6 10.2 %collective-permute-start.2 = (bf16[68,2,1024]{2,1,0:T(2,128)(2,1)S(1)}, bf16[68,2,1024]{2,1,0:T(2,128)(2,1)S(1)}, u32[]{:S(2)}, u32[]{:S(2)}) collective-permute-start(bf16[68,2,1024]{2,1,0:T(2,128)(2,1)S(1)} %get-tuple-element.8), channel_id=1, source_target_pairs={{0,1},{1,2},{2,3},{3,4},{4,5},{5,6},{6,7},{7,8},{8,9},{9,10},{10,1... | collective-permute-start | bytes 835592 | tf_op jit(solution)/shard_map/ppermute | solution.py:18
  16.3 9.1 %collective-permute-start.3 = (bf16[68,2,1024]{2,1,0:T(2,128)(2,1)S(1)}, bf16[68,2,1024]{2,1,0:T(2,128)(2,1)S(1)}, u32[]{:S(2)}, u32[]{:S(2)}) collective-permute-start(bf16[68,2,1024]{2,1,0:T(2,128)(2,1)S(1)} %get-tuple-element.9), channel_id=1, source_target_pairs={{1,0},{2,1},{3,2},{4,3},{5,4},{6,5},{7,6},{8,7},{9,8},{10,9},{11,1... | collective-permute-start | bytes 835592 | tf_op jit(solution)/shard_map/ppermute | solution.py:19
  27.1 2.8 %copy-start = (f32[68,20,1024]{2,1,0:T(8,128)}, f32[68,20,1024]{2,1,0:T(8,128)S(1)}, u32[]{:S(2)}) copy-start(f32[68,20,1024]{2,1,0:T(8,128)S(1)} %maximum_convert_fusion) | copy-start | bytes 16711684
  79.6 19.2 %all-to-all-start = ((f32[16,1,1024]{2,1,0:T(1,128)}), f32[16,1,1024]{2,1,0:T(1,128)S(1)}, u32[]{:S(2)}, u32[]{:S(2)}) async-start(f32[16,1,1024]{2,1,0:T(1,128)} %reshape.34), calls=%async_computation | async-start | bytes 131072 | tf_op jit(solution)/shard_map/all_to_all | solution.py:64
  98.8 13.6 %all-to-all-start.1 = ((f32[16,1,3072]{2,1,0:T(1,128)}), f32[16,1,3072]{2,1,0:T(1,128)S(1)}, u32[]{:S(2)}, u32[]{:S(2)}) async-start(f32[16,1,3072]{2,1,0:T(1,128)} %reshape.36), calls=%async_computation.1 | async-start | bytes 393216 | tf_op jit(solution)/shard_map/all_to_all | solution.py:57
where the time goes:
time: 119 us
  other arithmetic  56.5 us (47%)
  starting transfers between devices  27.8 us (23%)
  local copies, waits for them, and re-layouts  21.1 us (18%)
  waiting for transfers between devices  13.3 us (11%)
    another operation x1, other arithmetic, render(): running = jnp.cumsum(optical, axis=0)  42.3 us
    unnamed x9, local copies, waits for them, and re-layouts  11.7 us
    ppermute x2, starting transfers between devices, extended(): before = lax.ppermute(last, axis, up)  9.95 us
    unnamed x2, other arithmetic  8.43 us
    all_to_all x1, starting transfers between devices, body(): lax.all_to_all(transmit.reshape(1, 1, rows_here, cols_all), 'depth', spli...  7.97 us
    ppermute x2, waiting for transfers between devices, extended(): after = lax.ppermute(leading, axis, down)  7.52 us
    all_to_all x1, starting transfers between devices, body(): lax.all_to_all(color.reshape(3, 1, rows_here, cols_all), 'depth', split_a...  6.65 us
    all_to_all x1, waiting for transfers between devices, body(): lax.all_to_all(color.reshape(3, 1, rows_here, cols_all), 'depth', split_a...  4.24 us
  transfers between devices with their start and end apart: 6, of which 4 were waited for; matrix products, arithmetic and copies ran while one was open for 13% of the time, Pallas kernels for 0%

commit v1 on v0

v1 whole, which is shorter than its diff:
```python
import functools
import math

import jax
import jax.numpy as jnp
from jax import lax
from jax.experimental import pallas as pl
from jax.experimental.pallas import tpu as pltpu
from jax.sharding import PartitionSpec as P

MESH = pl.DeviceIdType.MESH
LC = 256
OW = 64
ZB = 8
PAD = 128
BASE = 0.15 * 3.0 / 0.85
GAIN = 0.85 / 3.0


def taps(delta):
    value = jnp.where(delta == -2, 1.0, 0.0)
    value = jnp.where(delta == -1, -8.0, value)
    value = jnp.where(delta == 1, 8.0, value)
    return jnp.where(delta == 2, -1.0, value)


def stencil_zx():
    shape = (128, 256)
    out = lax.broadcasted_iota(jnp.int32, shape, 0)
    col = lax.broadcasted_iota(jnp.int32, shape, 1)
    zo, xo = out >> 4, out & 15
    zi, xi = (col >> 4) - 2, col & 15
    inside = col < 192
    gz = jnp.where(inside & (xi == xo), taps(zi - zo), 0.0)
    gx = jnp.where(inside & (zi == zo), taps(xi - xo), 0.0)
    k = col - 192
    right = k >= 16
    k = k & 15
    near = (col >= 192) & (col < 224) & ((k >> 1) == zo)
    pos = (k & 1) + jnp.where(right, 16, -2)
    gx = gx + jnp.where(near, taps(pos - xo), 0.0)
    return gx, gz, gx + 2.0 * gz


def kernel(nd, nt, v_ref, o_ref, vp, xhl, xhr, elo, ehi, gy2, gyq, wt, ss, dzx, dy, sb, rb,
           load_sem, zs, zr, xs, xr, cs, cr):
    nz, cx, ny = v_ref.shape
    nc = ny // LC
    per = LC // OW
    d = lax.axis_index("depth")
    t = lax.axis_index("tile")
    step = 1.0 / (nz * nd)
    scale = step * math.log2(math.e)

    barrier = pltpu.get_barrier_semaphore()
    for i in range(1, nd):
        pl.semaphore_signal(barrier, inc=1, device_id=(lax.rem(d + i, nd), t), device_id_type=MESH)

    @pl.when(t > 0)
    def _():
        pl.semaphore_signal(barrier, inc=1, device_id=(d, t - 1), device_id_type=MESH)

    @pl.when(t < nt - 1)
    def _():
        pl.semaphore_signal(barrier, inc=1, device_id=(d, t + 1), device_id_type=MESH)

    def chunk(k):
        return lax.rem(d // per + 1 + k, nc)

    def load(k):
        lane = pl.multiple_of(chunk(k) * LC, LC)
        return pltpu.make_async_copy(
            v_ref.at[:, :, pl.ds(lane, LC)],
            vp.at[pl.ds(2, nz), :, pl.ds(pl.multiple_of(lane + PAD, PAD), LC)],
            load_sem.at[k],
        )

    for k in range(nc):
        load(k).start()

    zeros = jnp.zeros((nz, cx, PAD), jnp.bfloat16)
    vp[2 : 2 + nz, :, 0:PAD] = zeros
    vp[2 : 2 + nz, :, PAD + ny :] = zeros

    @pl.when(d == 0)
    def _():
        vp[0:2] = jnp.zeros((2, cx, ny + 2 * PAD), jnp.bfloat16)

    @pl.when(d == nd - 1)
    def _():
        vp[nz + 2 :] = jnp.zeros((2, cx, ny + 2 * PAD), jnp.bfloat16)

    @pl.when(t == 0)
    def _():
        xhl[...] = jnp.zeros(xhl.shape, jnp.bfloat16)

    @pl.when(t == nt - 1)
    def _():
        xhr[...] = jnp.zeros(xhr.shape, jnp.bfloat16)

    gx, gz, both = stencil_zx()
    dzx[0:128] = gx.astype(jnp.bfloat16)
    dzx[128:256] = gz.astype(jnp.bfloat16)
    dzx[256:384] = both.astype(jnp.bfloat16)
    src = lax.broadcasted_iota(jnp.int32, (LC + 2 * PAD, LC), 0)
    dst = lax.broadcasted_iota(jnp.int32, (LC + 2 * PAD, LC), 1)
    dy[...] = (2.0 * taps(src - PAD - dst)).astype(jnp.bfloat16)

    def z_up():
        return pltpu.make_async_remote_copy(
            src_ref=v_ref.at[pl.ds(nz - 2, 2)],
            dst_ref=vp.at[pl.ds(0, 2), :, pl.ds(PAD, ny)],
            send_sem=zs.at[0], recv_sem=zr.at[0],
            device_id=(lax.rem(d + 1, nd), t), device_id_type=MESH,
        )

    def z_down():
        return pltpu.make_async_remote_copy(
            src_ref=v_ref.at[pl.ds(0, 2)],
            dst_ref=vp.at[pl.ds(nz + 2, 2), :, pl.ds(PAD, ny)],
            send_sem=zs.at[1], recv_sem=zr.at[1],
            device_id=(lax.rem(d + nd - 1, nd), t), device_id_type=MESH,
        )

    def x_up(k):
        lane = pl.ds(pl.multiple_of(chunk(k) * LC, LC), LC)
        return pltpu.make_async_remote_copy(
            src_ref=ehi.at[:, lane], dst_ref=xhl.at[:, lane],
            send_sem=xs.at[0, k], recv_sem=xr.at[0, k],
            device_id=(d, lax.rem(t + 1, nt)), device_id_type=MESH,
        )

    def x_down(k):
        lane = pl.ds(pl.multiple_of(chunk(k) * LC, LC), LC)
        return pltpu.make_async_remote_copy(
            src_ref=elo.at[:, lane], dst_ref=xhr.at[:, lane],
            send_sem=xs.at[1, k], recv_sem=xr.at[1, k],
            device_id=(d, lax.rem(t + nt - 1, nt)), device_id_type=MESH,
        )

    for k in range(nc):
        load(k).wait()
        lane = pl.multiple_of(chunk(k) * LC, LC)
        rows = vp[2 : 2 + nz, :, pl.ds(pl.multiple_of(lane + PAD, PAD), LC)]
        elo[:, pl.ds(lane, LC)] = rows[:, 0:2].reshape(nz * 2, LC)
        ehi[:, pl.ds(lane, LC)] = rows[:, cx - 2 : cx].reshape(nz * 2, LC)
        if k == 0:
            waits = nd - 1 + (t > 0).astype(jnp.int32) + (t < nt - 1).astype(jnp.int32)
            pl.semaphore_wait(barrier, waits)

            @pl.when(d < nd - 1)
            def _():
                z_up().start()

            @pl.when(d > 0)
            def _():
                z_down().start()

        @pl.when(t < nt - 1)
        def _():
            x_up(k).start()

        @pl.when(t > 0)
        def _():
            x_down(k).start()

    def before_halo(k, _):
        lane = pl.multiple_of(chunk(k) * LC, LC)
        total = jnp.zeros((cx, LC), jnp.float32)
        last = jnp.ones((cx, LC), jnp.float32)
        part = min(256 // cx, nz)
        for z0 in range(0, nz, part):
            slab = vp[2 + z0 : 2 + z0 + part, :, pl.ds(lane, LC + 2 * PAD)]
            slab = slab.reshape(part * cx, LC + 2 * PAD)
            g = jnp.dot(slab, dy[...], preferred_element_type=jnp.float32)
            gy2[k, z0 * cx : (z0 + part) * cx] = g
            gyq[k, z0 * cx : (z0 + part) * cx] = g * g * 0.25 + 144.0
            for z in range(z0, z0 + part):
                f = vp[2 + z, :, pl.ds(pl.multiple_of(lane + PAD, PAD), LC)].astype(jnp.float32)
                total = total + f * f
                now = jnp.exp2(total * -scale - scale * (z + 1))
                wt[k, z * cx : (z + 1) * cx] = last - now
                last = now
        ss[k] = total * scale + scale * nz
        return 0

    lax.fori_loop(0, nc, before_halo, 0)

    @pl.when(d > 0)
    def _():
        z_up().wait_recv()

    @pl.when(d < nd - 1)
    def _():
        z_down().wait_recv()

    low = lax.broadcasted_iota(jnp.int32, (cx, 128), 1) < OW

    def send(owner):
        return pltpu.make_async_remote_copy(
            src_ref=sb.at[owner], dst_ref=rb.at[d],
            send_sem=cs.at[owner], recv_sem=cr.at[d],
            device_id=(owner, t), device_id_type=MESH,
        )

    def after_halo(k, _):
        @pl.when(t > 0)
        def _():
            x_up(k).wait_recv()

        @pl.when(t < nt - 1)
        def _():
            x_down(k).wait_recv()

        lane = pl.multiple_of(chunk(k) * LC, LC)
        inner = pl.multiple_of(lane + PAD, PAD)
        m0 = jnp.zeros((cx, LC), jnp.float32)
        m1 = m0
        m2 = m0
        for z0 in range(0, nz, ZB):
            slab = jnp.concatenate(
                [
                    vp[z0 : z0 + ZB + 4, :, pl.ds(inner, LC)].reshape((ZB + 4) * cx, LC),
                    xhl[z0 * 2 : (z0 + ZB) * 2, pl.ds(lane, LC)],
                    xhr[z0 * 2 : (z0 + ZB) * 2, pl.ds(lane, LC)],
                    jnp.zeros((32, LC), jnp.bfloat16),
                ],
                axis=0,
            )
            g = jnp.dot(dzx[...], slab, preferred_element_type=jnp.float32)
            for j in range(ZB):
                here = slice((z0 + j) * cx, (z0 + j + 1) * cx)
                gx = g[j * cx : (j + 1) * cx]
                gz = g[128 + j * cx : 128 + (j + 1) * cx]
                facing = jnp.abs(g[256 + j * cx : 256 + (j + 1) * cx] + gy2[k, here])
                facing = facing * lax.rsqrt(gx * gx + gz * gz + gyq[k, here])
                w = wt[k, here] * (facing + BASE)
                f = vp[2 + z0 + j, :, pl.ds(inner, LC)].astype(jnp.float32)
                wf = w * f
                m0 = m0 + w
                m1 = m1 + wf
                m2 = m2 + wf * f
        s = ss[k]
        for q in range(per):
            owner = chunk(k) * per + q
            part = slice((q // 2) * 128, (q // 2 + 1) * 128)
            a, b, c, e = m0[:, part], m1[:, part], m2[:, part], s[:, part]
            if q % 2 == 0:
                first = jnp.where(low, a, pltpu.roll(b, OW, 1))
                second = jnp.where(low, c, pltpu.roll(e, OW, 1))
            else:
                first = jnp.where(low, pltpu.roll(a, OW, 1), b)
                second = jnp.where(low, pltpu.roll(c, OW, 1), e)
            sb[owner, 0] = first
            sb[owner, 1] = second

            @pl.when(owner != d)
            def _():
                send(owner).start()

        return 0

    lax.fori_loop(0, nc, after_halo, 0)
    rb[d] = sb[d]

    for i in range(nd):

        @pl.when(d != i)
        def _():
            pltpu.make_async_remote_copy(
                src_ref=sb.at[i], dst_ref=rb.at[i],
                send_sem=cs.at[i], recv_sem=cr.at[i],
                device_id=(d, t), device_id_type=MESH,
            ).wait_recv()

    ahead = jnp.zeros((cx, 128), jnp.float32)
    acc0 = ahead
    acc1 = ahead
    for i in range(nd):
        p0, p1 = rb[i, 0], rb[i, 1]
        through = jnp.exp2(-ahead)
        acc0 = acc0 + through * p0
        acc1 = acc1 + through * p1
        ahead = ahead + jnp.where(low, pltpu.roll(p1, OW, 1), p1)
    a = acc0 * GAIN
    b = pltpu.roll(a, OW, 1)
    c = acc1 * GAIN
    o_ref[0] = (a + 0.5 * b)[:, :OW]
    o_ref[1] = (a - 0.3 * b + 0.2 * c)[:, :OW]
    o_ref[2] = (a + 0.25 * b - 0.1 * c)[:, :OW]
    o_ref[3] = (1.0 - jnp.exp2(-ahead))[:, :OW]

    @pl.when(d < nd - 1)
    def _():
        z_up().wait_send()

    @pl.when(d > 0)
    def _():
        z_down().wait_send()

    for k in range(nc):

        @pl.when(t < nt - 1)
        def _():
            x_up(k).wait_send()

        @pl.when(t > 0)
        def _():
            x_down(k).wait_send()

    for i in range(nd):

        @pl.when(d != i)
        def _():
            send(i).wait_send()


def solution(mesh):
    nd, nt = mesh.shape["depth"], mesh.shape["tile"]

    def body(volume):
        nz, cx, ny = volume.shape
        nc = ny // LC
        big = (nc, nz * cx, LC)
        return pl.pallas_call(
            functools.partial(kernel, nd, nt),
            out_shape=jax.ShapeDtypeStruct((4, cx, OW), jnp.float32),
            in_specs=[pl.BlockSpec(memory_space=pl.ANY)],
            out_specs=pl.BlockSpec(memory_space=pltpu.VMEM),
            scratch_shapes=[
                pltpu.VMEM((nz + 4, cx, ny + 2 * PAD), jnp.bfloat16),
                pltpu.VMEM((nz * 2, ny), jnp.bfloat16),
                pltpu.VMEM((nz * 2, ny), jnp.bfloat16),
                pltpu.VMEM((nz * 2, ny), jnp.bfloat16),
                pltpu.VMEM((nz * 2, ny), jnp.bfloat16),
                pltpu.VMEM(big, jnp.float32),
                pltpu.VMEM(big, jnp.float32),
                pltpu.VMEM(big, jnp.float32),
                pltpu.VMEM((nc, cx, LC), jnp.float32),
                pltpu.VMEM((384, 256), jnp.bfloat16),
                pltpu.VMEM((LC + 2 * PAD, LC), jnp.bfloat16),
                pltpu.VMEM((nd, 2, cx, 128), jnp.float32),
                pltpu.VMEM((nd, 2, cx, 128), jnp.float32),
                pltpu.SemaphoreType.DMA((nc,)),
                pltpu.SemaphoreType.DMA((2,)),
                pltpu.SemaphoreType.DMA((2,)),
                pltpu.SemaphoreType.DMA((2, nc)),
                pltpu.SemaphoreType.DMA((2, nc)),
                pltpu.SemaphoreType.DMA((nd,)),
                pltpu.SemaphoreType.DMA((nd,)),
            ],
            compiler_params=pltpu.CompilerParams(
                collective_id=0, has_side_effects=True, vmem_limit_bytes=60 * 2**20
            ),
        )(volume)

    return jax.shard_map(
        body,
        mesh=mesh,
        in_specs=(P("depth", "tile", None),),
        out_specs=P(None, "tile", "depth"),
        check_vma=False,
    )
```

time: 119 us -> 22.1 us (0.19)
  the two profiles are of different devices: /device:TPU:225 before, /device:TPU:2 now
where the time goes in v1:
time: 22.1 us; the launch traced here: 21.9 us
  Pallas kernels  20.5 us (93%)
  local copies, waits for them, and re-layouts  1.38 us (6%)
    pallas_call x1, Pallas kernels, body(): pl.pallas_call(functools.partial(kernel, nd, nt), out_shape=jax.ShapeDtyp...  20.5 us
    unnamed x1, local copies, waits for them, and re-layouts  1.38 us

profile of v1, /device:TPU:2, one launch (start us, length us, event | category | flops | bytes accessed | tf_op | source)
XLA Modules:
  0.0 21.9 jit_solution(6512936606968105336)
XLA Ops:
  0.0 20.5 %shard_map.17 = f32[4,16,64]{2,1,0:T(8,128)} custom-call(bf16[64,16,1024]{2,1,0:T(8,128)(2,1)} %v_ref.1), custom_call_target="tpu_custom_call" | custom-call | tf_op jit(solution)/shard_map/pallas_call | solution.py:325
  20.5 1.4 %copy.3 = f32[4,16,64]{2,1,0:T(8,128)} copy(f32[4,16,64]{2,1,0:T(8,128)} %shard_map.17) | data formatting | bytes 32768

commit v2 on v1

--- a/solution.py
+++ b/solution.py
@@ -3,6 +3,8 @@
 
 import jax
 import jax.numpy as jnp
+import ml_dtypes
+import numpy as np
 from jax import lax
 from jax.experimental import pallas as pl
 from jax.experimental.pallas import tpu as pltpu
@@ -13,59 +15,48 @@
 OW = 64
 ZB = 8
 PAD = 128
-BASE = 0.15 * 3.0 / 0.85
-GAIN = 0.85 / 3.0
+BASE = 0.15 * 3.0 / 0.85 / math.sqrt(5.0)
+GAIN = 0.85 / 3.0 * math.sqrt(5.0)
 
 
 def taps(delta):
-    value = jnp.where(delta == -2, 1.0, 0.0)
-    value = jnp.where(delta == -1, -8.0, value)
-    value = jnp.where(delta == 1, 8.0, value)
-    return jnp.where(delta == 2, -1.0, value)
+    value = np.zeros(delta.shape, np.float32)
+    for offset, weight in ((-2, 1.0), (-1, -8.0), (1, 8.0), (2, -1.0)):
+        value[delta == offset] = weight
+    return value
 
 
 def stencil_zx():
-    shape = (128, 256)
-    out = lax.broadcasted_iota(jnp.int32, shape, 0)
-    col = lax.broadcasted_iota(jnp.int32, shape, 1)
-    zo, xo = out >> 4, out & 15
-    zi, xi = (col >> 4) - 2, col & 15
+    out, col = np.indices((128, 256))
+    zo, xo = out // 16, out % 16
+    zi, xi = col // 16 - 2, col % 16
     inside = col < 192
-    gz = jnp.where(inside & (xi == xo), taps(zi - zo), 0.0)
-    gx = jnp.where(inside & (zi == zo), taps(xi - xo), 0.0)
-    k = col - 192
-    right = k >= 16
-    k = k & 15
-    near = (col >= 192) & (col < 224) & ((k >> 1) == zo)
-    pos = (k & 1) + jnp.where(right, 16, -2)
-    gx = gx + jnp.where(near, taps(pos - xo), 0.0)
-    return gx, gz, gx + 2.0 * gz
-
-
-def kernel(nd, nt, v_ref, o_ref, vp, xhl, xhr, elo, ehi, gy2, gyq, wt, ss, dzx, dy, sb, rb,
-           load_sem, zs, zr, xs, xr, cs, cr):
+    gz = np.where(inside & (xi == xo), taps(zi - zo), 0.0)
+    gx = np.where(inside & (zi == zo), taps(xi - xo), 0.0)
+    k = (col - 192) % 16
+    near = (col >= 192) & (col < 224) & (k // 2 == zo)
+    pos = k % 2 + np.where(col >= 208, 16, -2)
+    gx = gx + np.where(near, taps(pos - xo), 0.0)
+    return np.concatenate([gx + 2.0 * gz, 2.0 * gx - gz], 0).astype(ml_dtypes.bfloat16)
+
+
+def stencil_y():
+    src, dst = np.indices((LC + 2 * PAD, LC))
+    return (2.0 * taps(src - PAD - dst)).astype(ml_dtypes.bfloat16)
+
+
+def kernel(nd, nt, v_ref, dzx_ref, dy_ref, o_ref, vp, xhl, xhr, elo, ehi, gy2, gyq, wt, ss, dzx, dy,
+           ysb, yrb, xsb, xrb, load_sem, mat_sem, zs, zr, xs, xr, ys, yr, cs, cr):
     nz, cx, ny = v_ref.shape
     nc = ny // LC
     per = LC // OW
     d = lax.axis_index("depth")
     t = lax.axis_index("tile")
-    step = 1.0 / (nz * nd)
-    scale = step * math.log2(math.e)
-
-    barrier = pltpu.get_barrier_semaphore()
-    for i in range(1, nd):
-        pl.semaphore_signal(barrier, inc=1, device_id=(lax.rem(d + i, nd), t), device_id_type=MESH)
-
-    @pl.when(t > 0)
-    def _():
-        pl.semaphore_signal(barrier, inc=1, device_id=(d, t - 1), device_id_type=MESH)
-
-    @pl.when(t < nt - 1)
-    def _():
-        pl.semaphore_signal(barrier, inc=1, device_id=(d, t + 1), device_id_type=MESH)
+    row, col = d // per, lax.rem(d, per)
+    scale = math.log2(math.e) / (nz * nd)
 
     def chunk(k):
-        return lax.rem(d // per + 1 + k, nc)
+        return lax.rem(row + 1 + k, nc)
 
     def load(k):
         lane = pl.multiple_of(chunk(k) * LC, LC)
@@ -77,6 +68,41 @@
 
     for k in range(nc):
         load(k).start()
+    mats = (
+        pltpu.make_async_copy(dy_ref, dy, mat_sem.at[0]),
+        pltpu.make_async_copy(dzx_ref, dzx, mat_sem.at[1]),
+    )
+    for copy in mats:
+        copy.start()
+
+    barrier = pltpu.get_barrier_semaphore()
+
+    def greet(depth, tile):
+        pl.semaphore_signal(barrier, inc=1, device_id=(depth, tile), device_id_type=MESH)
+
+    @pl.when(t > 0)
+    def _():
+        greet(d, t - 1)
+
+    @pl.when(t < nt - 1)
+    def _():
+        greet(d, t + 1)
+
+    crosses_up = (col == per - 1) & (d < nd - 1)
+    crosses_down = (col == 0) & (d > 0)
+
+    @pl.when(crosses_up)
+    def _():
+        greet(d + 1, t)
+
+    @pl.when(crosses_down)
+    def _():
+        greet(d - 1, t)
+
+    for i in range(1, per):
+        greet(row * per + lax.rem(col + i, per), t)
+    for i in range(1, nc):
+        greet(lax.rem(row + i, nc) * per + col, t)
 
     zeros = jnp.zeros((nz, cx, PAD), jnp.bfloat16)
     vp[2 : 2 + nz, :, 0:PAD] = zeros
@@ -97,14 +123,6 @@
     @pl.when(t == nt - 1)
     def _():
         xhr[...] = jnp.zeros(xhr.shape, jnp.bfloat16)
-
-    gx, gz, both = stencil_zx()
-    dzx[0:128] = gx.astype(jnp.bfloat16)
-    dzx[128:256] = gz.astype(jnp.bfloat16)
-    dzx[256:384] = both.astype(jnp.bfloat16)
-    src = lax.broadcasted_iota(jnp.int32, (LC + 2 * PAD, LC), 0)
-    dst = lax.broadcasted_iota(jnp.int32, (LC + 2 * PAD, LC), 1)
-    dy[...] = (2.0 * taps(src - PAD - dst)).astype(jnp.bfloat16)
 
     def z_up():
         return pltpu.make_async_remote_copy(
@@ -145,7 +163,9 @@
         elo[:, pl.ds(lane, LC)] = rows[:, 0:2].reshape(nz * 2, LC)
         ehi[:, pl.ds(lane, LC)] = rows[:, cx - 2 : cx].reshape(nz * 2, LC)
         if k == 0:
-            waits = nd - 1 + (t > 0).astype(jnp.int32) + (t < nt - 1).astype(jnp.int32)
+            waits = per - 1 + nc - 1
+            for there in (t > 0, t < nt - 1, crosses_up, crosses_down):
+                waits = waits + there.astype(jnp.int32)
             pl.semaphore_wait(barrier, waits)
 
             @pl.when(d < nd - 1)
@@ -163,6 +183,9 @@
         @pl.when(t > 0)
         def _():
             x_down(k).start()
+
+    for copy in mats:
+        copy.wait()
 
     def before_halo(k, _):
         lane = pl.multiple_of(chunk(k) * LC, LC)
@@ -174,7 +197,7 @@
             slab = slab.reshape(part * cx, LC + 2 * PAD)
             g = jnp.dot(slab, dy[...], preferred_element_type=jnp.float32)
             gy2[k, z0 * cx : (z0 + part) * cx] = g
-            gyq[k, z0 * cx : (z0 + part) * cx] = g * g * 0.25 + 144.0
+            gyq[k, z0 * cx : (z0 + part) * cx] = g * g * 1.25 + 720.0
             for z in range(z0, z0 + part):
                 f = vp[2 + z, :, pl.ds(pl.multiple_of(lane + PAD, PAD), LC)].astype(jnp.float32)
                 total = total + f * f
@@ -196,12 +219,53 @@
 
     low = lax.broadcasted_iota(jnp.int32, (cx, 128), 1) < OW
 
-    def send(owner):
-        return pltpu.make_async_remote_copy(
-            src_ref=sb.at[owner], dst_ref=rb.at[d],
-            send_sem=cs.at[owner], recv_sem=cr.at[d],
-            device_id=(owner, t), device_id_type=MESH,
-        )
+    def y_send(k, q):
+        return pltpu.make_async_remote_copy(
+            src_ref=ysb.at[k, q], dst_ref=yrb.at[k, col],
+            send_sem=ys.at[k, q], recv_sem=yr.at[k, col],
+            device_id=(row * per + q, t), device_id_type=MESH,
+        )
+
+    def y_arrival(k, q):
+        return pltpu.make_async_remote_copy(
+            src_ref=ysb.at[k, q], dst_ref=yrb.at[k, q],
+            send_sem=ys.at[k, q], recv_sem=yr.at[k, q],
+            device_id=(d, t), device_id_type=MESH,
+        )
+
+    def x_send(k):
+        return pltpu.make_async_remote_copy(
+            src_ref=xsb.at[k], dst_ref=xrb.at[row],
+            send_sem=cs.at[k], recv_sem=cr.at[row],
+            device_id=(chunk(k) * per + col, t), device_id_type=MESH,
+        )
+
+    def x_arrival(r):
+        return pltpu.make_async_remote_copy(
+            src_ref=xsb.at[0], dst_ref=xrb.at[r],
+            send_sem=cs.at[0], recv_sem=cr.at[r],
+            device_id=(d, t), device_id_type=MESH,
+        )
+
+    def composite(parts):
+        ahead = jnp.zeros((cx, 128), jnp.float32)
+        acc0 = ahead
+        acc1 = ahead
+        for p0, p1 in parts:
+            through = jnp.exp2(-ahead)
+            acc0 = acc0 + through * p0
+            acc1 = acc1 + through * p1
+            ahead = ahead + jnp.where(low, pltpu.roll(p1, OW, 1), p1)
+        return acc0, acc1, ahead
+
+    def join_row(k):
+        for q in range(per):
+
+            @pl.when(q != col)
+            def _():
+                y_arrival(k, q).wait_recv()
+
+        return composite([(yrb[k, q, 0], yrb[k, q, 1]) for q in range(per)])
 
     def after_halo(k, _):
         @pl.when(t > 0)
@@ -230,10 +294,10 @@
             g = jnp.dot(dzx[...], slab, preferred_element_type=jnp.float32)
             for j in range(ZB):
                 here = slice((z0 + j) * cx, (z0 + j + 1) * cx)
-                gx = g[j * cx : (j + 1) * cx]
-                gz = g[128 + j * cx : 128 + (j + 1) * cx]
-                facing = jnp.abs(g[256 + j * cx : 256 + (j + 1) * cx] + gy2[k, here])
-                facing = facing * lax.rsqrt(gx * gx + gz * gz + gyq[k, here])
+                p = g[j * cx : (j + 1) * cx]
+                q = g[128 + j * cx : 128 + (j + 1) * cx]
+                facing = jnp.abs(p + gy2[k, here])
+                facing = facing * lax.rsqrt(p * p + q * q + gyq[k, here])
                 w = wt[k, here] * (facing + BASE)
                 f = vp[2 + z0 + j, :, pl.ds(inner, LC)].astype(jnp.float32)
                 wf = w * f
@@ -242,7 +306,6 @@
                 m2 = m2 + wf * f
         s = ss[k]
         for q in range(per):
-            owner = chunk(k) * per + q
             part = slice((q // 2) * 128, (q // 2 + 1) * 128)
             a, b, c, e = m0[:, part], m1[:, part], m2[:, part], s[:, part]
             if q % 2 == 0:
@@ -251,37 +314,38 @@
             else:
                 first = jnp.where(low, pltpu.roll(a, OW, 1), b)
                 second = jnp.where(low, pltpu.roll(c, OW, 1), e)
-            sb[owner, 0] = first
-            sb[owner, 1] = second
-
-            @pl.when(owner != d)
-            def _():
-                send(owner).start()
+            ysb[k, q, 0] = first
+            ysb[k, q, 1] = second
+
+            @pl.when(q != col)
+            def _():
+                y_send(k, q).start()
+
+            @pl.when(q == col)
+            def _():
+                yrb[k, q, 0] = first
+                yrb[k, q, 1] = second
+
+        @pl.when(k > 0)
+        def _():
+            acc0, acc1, ahead = join_row(k - 1)
+            xsb[k - 1, 0] = acc0
+            xsb[k - 1, 1] = jnp.where(low, acc1, ahead)
+            x_send(k - 1).start()
 
         return 0
 
     lax.fori_loop(0, nc, after_halo, 0)
-    rb[d] = sb[d]
-
-    for i in range(nd):
-
-        @pl.when(d != i)
-        def _():
-            pltpu.make_async_remote_copy(
-                src_ref=sb.at[i], dst_ref=rb.at[i],
-                send_sem=cs.at[i], recv_sem=cr.at[i],
-                device_id=(d, t), device_id_type=MESH,
-            ).wait_recv()
-
-    ahead = jnp.zeros((cx, 128), jnp.float32)
-    acc0 = ahead
-    acc1 = ahead
-    for i in range(nd):
-        p0, p1 = rb[i, 0], rb[i, 1]
-        through = jnp.exp2(-ahead)
-        acc0 = acc0 + through * p0
-        acc1 = acc1 + through * p1
-        ahead = ahead + jnp.where(low, pltpu.roll(p1, OW, 1), p1)
+    acc0, acc1, ahead = join_row(nc - 1)
+    xrb[row, 0] = acc0
+    xrb[row, 1] = jnp.where(low, acc1, ahead)
+    for r in range(nc):
+
+        @pl.when(r != row)
+        def _():
+            x_arrival(r).wait_recv()
+
+    acc0, acc1, ahead = composite([(xrb[r, 0], xrb[r, 1]) for r in range(nc)])
     a = acc0 * GAIN
     b = pltpu.roll(a, OW, 1)
     c = acc1 * GAIN
@@ -308,11 +372,14 @@
         def _():
             x_down(k).wait_send()
 
-    for i in range(nd):
-
-        @pl.when(d != i)
-        def _():
-            send(i).wait_send()
+        for q in range(per):
+
+            @pl.when(q != col)
+            def _():
+                y_send(k, q).wait_send()
+
+        if k < nc - 1:
+            x_send(k).wait_send()
 
 
 def solution(mesh):
@@ -320,12 +387,12 @@
 
     def body(volume):
         nz, cx, ny = volume.shape
-        nc = ny // LC
+        nc, per = ny // LC, LC // OW
         big = (nc, nz * cx, LC)
         return pl.pallas_call(
             functools.partial(kernel, nd, nt),
             out_shape=jax.ShapeDtypeStruct((4, cx, OW), jnp.float32),
-            in_specs=[pl.BlockSpec(memory_space=pl.ANY)],
+            in_specs=[pl.BlockSpec(memory_space=pl.ANY)] * 3,
             out_specs=pl.BlockSpec(memory_space=pltpu.VMEM),
             scratch_shapes=[
                 pltpu.VMEM((nz + 4, cx, ny + 2 * PAD), jnp.bfloat16),
@@ -337,22 +404,27 @@
                 pltpu.VMEM(big, jnp.float32),
                 pltpu.VMEM(big, jnp.float32),
                 pltpu.VMEM((nc, cx, LC), jnp.float32),
-                pltpu.VMEM((384, 256), jnp.bfloat16),
+                pltpu.VMEM((256, 256), jnp.bfloat16),
                 pltpu.VMEM((LC + 2 * PAD, LC), jnp.bfloat16),
-                pltpu.VMEM((nd, 2, cx, 128), jnp.float32),
-                pltpu.VMEM((nd, 2, cx, 128), jnp.float32),
+                pltpu.VMEM((nc, per, 2, cx, 128), jnp.float32),
+                pltpu.VMEM((nc, per, 2, cx, 128), jnp.float32),
+                pltpu.VMEM((nc, 2, cx, 128), jnp.float32),
+                pltpu.VMEM((nc, 2, cx, 128), jnp.float32),
                 pltpu.SemaphoreType.DMA((nc,)),
+                pltpu.SemaphoreType.DMA((2,)),
                 pltpu.SemaphoreType.DMA((2,)),
                 pltpu.SemaphoreType.DMA((2,)),
                 pltpu.SemaphoreType.DMA((2, nc)),
                 pltpu.SemaphoreType.DMA((2, nc)),
-                pltpu.SemaphoreType.DMA((nd,)),
-                pltpu.SemaphoreType.DMA((nd,)),
+                pltpu.SemaphoreType.DMA((nc, per)),
+                pltpu.SemaphoreType.DMA((nc, per)),
+                pltpu.SemaphoreType.DMA((nc,)),
+                pltpu.SemaphoreType.DMA((nc,)),
             ],
             compiler_params=pltpu.CompilerParams(
                 collective_id=0, has_side_effects=True, vmem_limit_bytes=60 * 2**20
             ),
-        )(volume)
+        )(volume, jnp.asarray(stencil_zx()), jnp.asarray(stencil_y()))
 
     return jax.shard_map(
         body,

time: 22.1 us -> 26.6 us (1.20)
  Pallas kernels: 20.5 us -> 25 us
    pallas_call x1, Pallas kernels: 20.5 us -> 25 us  [body(): pl.pallas_call(functools.partial(kernel, nd, nt), out_shape=jax.ShapeDtyp...]
where the time goes in v2:
time: 26.6 us; the launch traced here: 26.4 us
  Pallas kernels  25 us (94%)
  local copies, waits for them, and re-layouts  1.38 us (5%)
    pallas_call x1, Pallas kernels, body(): pl.pallas_call(functools.partial(kernel, nd, nt), out_shape=jax.ShapeDtyp...  25 us
    unnamed x1, local copies, waits for them, and re-layouts  1.38 us

profile of v2, /device:TPU:2, one launch (start us, length us, event | category | flops | bytes accessed | tf_op | source)
XLA Modules:
  0.0 26.4 jit_solution(14968701455156802471)
XLA Ops:
  0.0 25.0 %shard_map.37 = f32[4,16,64]{2,1,0:T(8,128)} custom-call(bf16[64,16,1024]{2,1,0:T(8,128)(2,1)} %v_ref.1, bf16[256,256]{1,0:T(8,128)(2,1)} %constant.4.clone.dzx_ref, bf16[512,256]{1,0:T(8,128)(2,1)} %constant.5.clone.dy_ref), custom_call_target="tpu_custom_call" | custom-call | tf_op jit(solution)/shard_map/pallas_call | solution.py:392
  25.0 1.4 %copy.5 = f32[4,16,64]{2,1,0:T(8,128)} copy(f32[4,16,64]{2,1,0:T(8,128)} %shard_map.37) | data formatting | bytes 32768

commit v3 on v2

--- a/solution.py
+++ b/solution.py
@@ -16,6 +16,7 @@
 ZB = 8
 PAD = 128
 BASE = 0.15 * 3.0 / 0.85 / math.sqrt(5.0)
+CODE = 44.0
 GAIN = 0.85 / 3.0 * math.sqrt(5.0)
 
 
@@ -45,8 +46,21 @@
     return (2.0 * taps(src - PAD - dst)).astype(ml_dtypes.bfloat16)
 
 
+def encode(value):
+    v = value * CODE
+    v2 = v * v
+    v4 = v2 * v2
+    return (v4 * v4 * v2 * v).astype(jnp.bfloat16)
+
+
+def decode(code):
+    u = code.astype(jnp.float32)
+    size = jnp.exp2(jnp.log2(jnp.maximum(jnp.abs(u), 1e-37)) * (1.0 / 11.0) - math.log2(CODE))
+    return jnp.where(u < 0.0, -size, size)
+
+
 def kernel(nd, nt, v_ref, dzx_ref, dy_ref, o_ref, vp, xhl, xhr, elo, ehi, gy2, gyq, wt, ss, dzx, dy,
-           ysb, yrb, xsb, xrb, load_sem, mat_sem, zs, zr, xs, xr, ys, yr, cs, cr):
+           sb, rb, got, load_sem, mat_sem, zs, zr, xs, xr, cs, cr):
     nz, cx, ny = v_ref.shape
     nc = ny // LC
     per = LC // OW
@@ -56,7 +70,11 @@
     scale = math.log2(math.e) / (nz * nd)
 
     def chunk(k):
-        return lax.rem(row + 1 + k, nc)
+        if nc != 4:
+            return lax.rem(row + 1 + k, nc)
+        if isinstance(k, int):
+            return lax.rem(row + (2, 1, 3, 0)[k], nc)
+        return lax.rem(row + jnp.where(k == 3, 0, jnp.where(k == 2, 3, 2 - k)), nc)
 
     def load(k):
         lane = pl.multiple_of(chunk(k) * LC, LC)
@@ -88,21 +106,8 @@
     def _():
         greet(d, t + 1)
 
-    crosses_up = (col == per - 1) & (d < nd - 1)
-    crosses_down = (col == 0) & (d > 0)
-
-    @pl.when(crosses_up)
-    def _():
-        greet(d + 1, t)
-
-    @pl.when(crosses_down)
-    def _():
-        greet(d - 1, t)
-
-    for i in range(1, per):
-        greet(row * per + lax.rem(col + i, per), t)
-    for i in range(1, nc):
-        greet(lax.rem(row + i, nc) * per + col, t)
+    for i in (1, nd - 1, *range(2, nd - 1)):
+        greet(lax.rem(d + i, nd), t)
 
     zeros = jnp.zeros((nz, cx, PAD), jnp.bfloat16)
     vp[2 : 2 + nz, :, 0:PAD] = zeros
@@ -163,9 +168,7 @@
         elo[:, pl.ds(lane, LC)] = rows[:, 0:2].reshape(nz * 2, LC)
         ehi[:, pl.ds(lane, LC)] = rows[:, cx - 2 : cx].reshape(nz * 2, LC)
         if k == 0:
-            waits = per - 1 + nc - 1
-            for there in (t > 0, t < nt - 1, crosses_up, crosses_down):
-                waits = waits + there.astype(jnp.int32)
+            waits = nd - 1 + (t > 0).astype(jnp.int32) + (t < nt - 1).astype(jnp.int32)
             pl.semaphore_wait(barrier, waits)
 
             @pl.when(d < nd - 1)
@@ -219,53 +222,19 @@
 
     low = lax.broadcasted_iota(jnp.int32, (cx, 128), 1) < OW
 
-    def y_send(k, q):
-        return pltpu.make_async_remote_copy(
-            src_ref=ysb.at[k, q], dst_ref=yrb.at[k, col],
-            send_sem=ys.at[k, q], recv_sem=yr.at[k, col],
-            device_id=(row * per + q, t), device_id_type=MESH,
-        )
-
-    def y_arrival(k, q):
-        return pltpu.make_async_remote_copy(
-            src_ref=ysb.at[k, q], dst_ref=yrb.at[k, q],
-            send_sem=ys.at[k, q], recv_sem=yr.at[k, q],
+    def send(owner):
+        return pltpu.make_async_remote_copy(
+            src_ref=sb.at[owner], dst_ref=rb.at[d],
+            send_sem=cs.at[owner], recv_sem=cr.at[d],
+            device_id=(owner, t), device_id_type=MESH,
+        )
+
+    def arrival(i):
+        return pltpu.make_async_remote_copy(
+            src_ref=sb.at[i], dst_ref=rb.at[i],
+            send_sem=cs.at[i], recv_sem=cr.at[i],
             device_id=(d, t), device_id_type=MESH,
         )
-
-    def x_send(k):
-        return pltpu.make_async_remote_copy(
-            src_ref=xsb.at[k], dst_ref=xrb.at[row],
-            send_sem=cs.at[k], recv_sem=cr.at[row],
-            device_id=(chunk(k) * per + col, t), device_id_type=MESH,
-        )
-
-    def x_arrival(r):
-        return pltpu.make_async_remote_copy(
-            src_ref=xsb.at[0], dst_ref=xrb.at[r],
-            send_sem=cs.at[0], recv_sem=cr.at[r],
-            device_id=(d, t), device_id_type=MESH,
-        )
-
-    def composite(parts):
-        ahead = jnp.zeros((cx, 128), jnp.float32)
-        acc0 = ahead
-        acc1 = ahead
-        for p0, p1 in parts:
-            through = jnp.exp2(-ahead)
-            acc0 = acc0 + through * p0
-            acc1 = acc1 + through * p1
-            ahead = ahead + jnp.where(low, pltpu.roll(p1, OW, 1), p1)
-        return acc0, acc1, ahead
-
-    def join_row(k):
-        for q in range(per):
-
-            @pl.when(q != col)
-            def _():
-                y_arrival(k, q).wait_recv()
-
-        return composite([(yrb[k, q, 0], yrb[k, q, 1]) for q in range(per)])
 
     def after_halo(k, _):
         @pl.when(t > 0)
@@ -314,38 +283,45 @@
             else:
                 first = jnp.where(low, pltpu.roll(a, OW, 1), b)
                 second = jnp.where(low, pltpu.roll(c, OW, 1), e)
-            ysb[k, q, 0] = first
-            ysb[k, q, 1] = second
-
-            @pl.when(q != col)
+            owner = chunk(k) * per + q
+
+            @pl.when(owner != d)
             def _():
-                y_send(k, q).start()
-
-            @pl.when(q == col)
+                sb[owner, 0] = encode(first)
+                sb[owner, 1] = encode(second)
+                send(owner).start()
+
+            @pl.when(owner == d)
             def _():
-                yrb[k, q, 0] = first
-                yrb[k, q, 1] = second
-
-        @pl.when(k > 0)
-        def _():
-            acc0, acc1, ahead = join_row(k - 1)
-            xsb[k - 1, 0] = acc0
-            xsb[k - 1, 1] = jnp.where(low, acc1, ahead)
-            x_send(k - 1).start()
+                got[d, 0] = first
+                got[d, 1] = second
 
         return 0
 
     lax.fori_loop(0, nc, after_halo, 0)
-    acc0, acc1, ahead = join_row(nc - 1)
-    xrb[row, 0] = acc0
-    xrb[row, 1] = jnp.where(low, acc1, ahead)
-    for r in range(nc):
-
-        @pl.when(r != row)
-        def _():
-            x_arrival(r).wait_recv()
-
-    acc0, acc1, ahead = composite([(xrb[r, 0], xrb[r, 1]) for r in range(nc)])
+
+    def take(r, q):
+        @pl.when((r != row) | (q != col))
+        def _():
+            i = r * per + q
+            arrival(i).wait_recv()
+            got[i] = decode(rb[i])
+
+    def other_row(n, _):
+        for q in range(per):
+            take(lax.rem(row + n, nc), q)
+        return 0
+
+    lax.fori_loop(1, nc + 1, other_row, 0)
+    ahead = jnp.zeros((cx, 128), jnp.float32)
+    acc0 = ahead
+    acc1 = ahead
+    for i in range(nd):
+        p0, p1 = got[i, 0], got[i, 1]
+        through = jnp.exp2(-ahead)
+        acc0 = acc0 + through * p0
+        acc1 = acc1 + through * p1
+        ahead = ahead + jnp.where(low, pltpu.roll(p1, OW, 1), p1)
     a = acc0 * GAIN
     b = pltpu.roll(a, OW, 1)
     c = acc1 * GAIN
@@ -372,14 +348,11 @@
         def _():
             x_down(k).wait_send()
 
-        for q in range(per):
-
-            @pl.when(q != col)
-            def _():
-                y_send(k, q).wait_send()
-
-        if k < nc - 1:
-            x_send(k).wait_send()
+    for i in range(nd):
+
+        @pl.when(d != i)
+        def _():
+            send(i).wait_send()
 
 
 def solution(mesh):
@@ -387,7 +360,7 @@
 
     def body(volume):
         nz, cx, ny = volume.shape
-        nc, per = ny // LC, LC // OW
+        nc = ny // LC
         big = (nc, nz * cx, LC)
         return pl.pallas_call(
             functools.partial(kernel, nd, nt),
@@ -406,20 +379,17 @@
                 pltpu.VMEM((nc, cx, LC), jnp.float32),
                 pltpu.VMEM((256, 256), jnp.bfloat16),
                 pltpu.VMEM((LC + 2 * PAD, LC), jnp.bfloat16),
-                pltpu.VMEM((nc, per, 2, cx, 128), jnp.float32),
-                pltpu.VMEM((nc, per, 2, cx, 128), jnp.float32),
-                pltpu.VMEM((nc, 2, cx, 128), jnp.float32),
-                pltpu.VMEM((nc, 2, cx, 128), jnp.float32),
+                pltpu.VMEM((nd, 2, cx, 128), jnp.bfloat16),
+                pltpu.VMEM((nd, 2, cx, 128), jnp.bfloat16),
+                pltpu.VMEM((nd, 2, cx, 128), jnp.float32),
                 pltpu.SemaphoreType.DMA((nc,)),
                 pltpu.SemaphoreType.DMA((2,)),
                 pltpu.SemaphoreType.DMA((2,)),
                 pltpu.SemaphoreType.DMA((2,)),
                 pltpu.SemaphoreType.DMA((2, nc)),
                 pltpu.SemaphoreType.DMA((2, nc)),
-                pltpu.SemaphoreType.DMA((nc, per)),
-                pltpu.SemaphoreType.DMA((nc, per)),
-                pltpu.SemaphoreType.DMA((nc,)),
-                pltpu.SemaphoreType.DMA((nc,)),
+                pltpu.SemaphoreType.DMA((nd,)),
+                pltpu.SemaphoreType.DMA((nd,)),
             ],
             compiler_params=pltpu.CompilerParams(
                 collective_id=0, has_side_effects=True, vmem_limit_bytes=60 * 2**20

time: 26.6 us -> 22.5 us (0.85)
  Pallas kernels: 25 us -> 20.9 us
    pallas_call x1, Pallas kernels: 25 us -> 20.9 us  [body(): pl.pallas_call(functools.partial(kernel, nd, nt), out_shape=jax.ShapeDtyp...]
where the time goes in v3:
time: 22.5 us; the launch traced here: 22.3 us
  Pallas kernels  20.9 us (93%)
  local copies, waits for them, and re-layouts  1.38 us (6%)
    pallas_call x1, Pallas kernels, body(): pl.pallas_call(functools.partial(kernel, nd, nt), out_shape=jax.ShapeDtyp...  20.9 us
    unnamed x1, local copies, waits for them, and re-layouts  1.38 us

profile of v3, /device:TPU:2, one launch (start us, length us, event | category | flops | bytes accessed | tf_op | source)
XLA Modules:
  0.0 22.3 jit_solution(1163570892156176005)
XLA Ops:
  0.0 20.9 %shard_map.37 = f32[4,16,64]{2,1,0:T(8,128)} custom-call(bf16[64,16,1024]{2,1,0:T(8,128)(2,1)} %v_ref.1, bf16[256,256]{1,0:T(8,128)(2,1)} %constant.4.clone.dzx_ref, bf16[512,256]{1,0:T(8,128)(2,1)} %constant.5.clone.dy_ref), custom_call_target="tpu_custom_call" | custom-call | tf_op jit(solution)/shard_map/pallas_call | solution.py:365
  20.9 1.4 %copy.5 = f32[4,16,64]{2,1,0:T(8,128)} copy(f32[4,16,64]{2,1,0:T(8,128)} %shard_map.37) | data formatting | bytes 32768

commit v4 on v3

--- a/solution.py
+++ b/solution.py
@@ -3,8 +3,6 @@
 
 import jax
 import jax.numpy as jnp
-import ml_dtypes
-import numpy as np
 from jax import lax
 from jax.experimental import pallas as pl
 from jax.experimental.pallas import tpu as pltpu
@@ -21,29 +19,24 @@
 
 
 def taps(delta):
-    value = np.zeros(delta.shape, np.float32)
-    for offset, weight in ((-2, 1.0), (-1, -8.0), (1, 8.0), (2, -1.0)):
-        value[delta == offset] = weight
-    return value
+    value = jnp.where(delta == -2, 1.0, 0.0)
+    value = jnp.where(delta == -1, -8.0, value)
+    value = jnp.where(delta == 1, 8.0, value)
+    return jnp.where(delta == 2, -1.0, value)
 
 
 def stencil_zx():
-    out, col = np.indices((128, 256))
-    zo, xo = out // 16, out % 16
-    zi, xi = col // 16 - 2, col % 16
+    out = lax.broadcasted_iota(jnp.int32, (128, 256), 0)
+    col = lax.broadcasted_iota(jnp.int32, (128, 256), 1)
+    zo, xo = out >> 4, out & 15
+    zi, xi = (col >> 4) - 2, col & 15
     inside = col < 192
-    gz = np.where(inside & (xi == xo), taps(zi - zo), 0.0)
-    gx = np.where(inside & (zi == zo), taps(xi - xo), 0.0)
-    k = (col - 192) % 16
-    near = (col >= 192) & (col < 224) & (k // 2 == zo)
-    pos = k % 2 + np.where(col >= 208, 16, -2)
-    gx = gx + np.where(near, taps(pos - xo), 0.0)
-    return np.concatenate([gx + 2.0 * gz, 2.0 * gx - gz], 0).astype(ml_dtypes.bfloat16)
-
-
-def stencil_y():
-    src, dst = np.indices((LC + 2 * PAD, LC))
-    return (2.0 * taps(src - PAD - dst)).astype(ml_dtypes.bfloat16)
+    gz = jnp.where(inside & (xi == xo), taps(zi - zo), 0.0)
+    k = col & 15
+    pos = (k & 1) + jnp.where(col >= 208, 16, -2)
+    plane = jnp.where(inside, zi, jnp.where(col < 224, k >> 1, -9))
+    gx = jnp.where(plane == zo, taps(jnp.where(inside, xi, pos) - xo), 0.0)
+    return gx + 2.0 * gz, 2.0 * gx - gz
 
 
 def encode(value):
@@ -59,8 +52,8 @@
     return jnp.where(u < 0.0, -size, size)
 
 
-def kernel(nd, nt, v_ref, dzx_ref, dy_ref, o_ref, vp, xhl, xhr, elo, ehi, gy2, gyq, wt, ss, dzx, dy,
-           sb, rb, got, load_sem, mat_sem, zs, zr, xs, xr, cs, cr):
+def kernel(nd, nt, v_ref, o_ref, vp, xhl, xhr, elo, ehi, gy2, gyq, wt, ss, dzx, dy,
+           sb, rb, got, gbuf, load_sem, zs, zr, xs, xr, cs, cr):
     nz, cx, ny = v_ref.shape
     nc = ny // LC
     per = LC // OW
@@ -69,12 +62,13 @@
     row, col = d // per, lax.rem(d, per)
     scale = math.log2(math.e) / (nz * nd)
 
-    def chunk(k):
+    def chunk(k, r=None):
+        r = row if r is None else r
         if nc != 4:
-            return lax.rem(row + 1 + k, nc)
+            return lax.rem(r + 1 + k, nc)
         if isinstance(k, int):
-            return lax.rem(row + (2, 1, 3, 0)[k], nc)
-        return lax.rem(row + jnp.where(k == 3, 0, jnp.where(k == 2, 3, 2 - k)), nc)
+            return lax.rem(r + (2, 1, 3, 0)[k], nc)
+        return lax.rem(r + jnp.where(k == 3, 0, jnp.where(k == 2, 3, 2 - k)), nc)
 
     def load(k):
         lane = pl.multiple_of(chunk(k) * LC, LC)
@@ -86,12 +80,6 @@
 
     for k in range(nc):
         load(k).start()
-    mats = (
-        pltpu.make_async_copy(dy_ref, dy, mat_sem.at[0]),
-        pltpu.make_async_copy(dzx_ref, dzx, mat_sem.at[1]),
-    )
-    for copy in mats:
-        copy.start()
 
     barrier = pltpu.get_barrier_semaphore()
 
@@ -129,20 +117,31 @@
     def _():
         xhr[...] = jnp.zeros(xhr.shape, jnp.bfloat16)
 
-    def z_up():
-        return pltpu.make_async_remote_copy(
-            src_ref=v_ref.at[pl.ds(nz - 2, 2)],
-            dst_ref=vp.at[pl.ds(0, 2), :, pl.ds(PAD, ny)],
-            send_sem=zs.at[0], recv_sem=zr.at[0],
-            device_id=(lax.rem(d + 1, nd), t), device_id_type=MESH,
-        )
-
-    def z_down():
-        return pltpu.make_async_remote_copy(
-            src_ref=v_ref.at[pl.ds(0, 2)],
-            dst_ref=vp.at[pl.ds(nz + 2, 2), :, pl.ds(PAD, ny)],
-            send_sem=zs.at[1], recv_sem=zr.at[1],
-            device_id=(lax.rem(d + nd - 1, nd), t), device_id_type=MESH,
+    p_taps, q_taps = stencil_zx()
+    dzx[0:128] = p_taps.astype(jnp.bfloat16)
+    dzx[128:256] = q_taps.astype(jnp.bfloat16)
+    src = lax.broadcasted_iota(jnp.int32, (PAD, LC), 0)
+    dst = lax.broadcasted_iota(jnp.int32, (PAD, LC), 1)
+    for i in range(0, LC + 2 * PAD, PAD):
+        dy[i : i + PAD] = (2.0 * taps(src - dst + (i - PAD))).astype(jnp.bfloat16)
+
+    def z_copy(k, up):
+        there = lax.rem(d + (1 if up else nd - 1), nd)
+        lane = pl.multiple_of(chunk(k, there // per) * LC, LC)
+        return pltpu.make_async_remote_copy(
+            src_ref=v_ref.at[pl.ds(nz - 2 if up else 0, 2), :, pl.ds(lane, LC)],
+            dst_ref=vp.at[pl.ds(0 if up else nz + 2, 2), :, pl.ds(pl.multiple_of(lane + PAD, PAD), LC)],
+            send_sem=zs.at[1 - up, k], recv_sem=zr.at[1 - up, k],
+            device_id=(there, t), device_id_type=MESH,
+        )
+
+    def z_arrival(k, up):
+        lane = pl.multiple_of(chunk(k) * LC, LC)
+        return pltpu.make_async_remote_copy(
+            src_ref=v_ref.at[pl.ds(0, 2), :, pl.ds(lane, LC)],
+            dst_ref=vp.at[pl.ds(0 if up else nz + 2, 2), :, pl.ds(pl.multiple_of(lane + PAD, PAD), LC)],
+            send_sem=zs.at[1 - up, k], recv_sem=zr.at[1 - up, k],
+            device_id=(d, t), device_id_type=MESH,
         )
 
     def x_up(k):
@@ -171,14 +170,6 @@
             waits = nd - 1 + (t > 0).astype(jnp.int32) + (t < nt - 1).astype(jnp.int32)
             pl.semaphore_wait(barrier, waits)
 
-            @pl.when(d < nd - 1)
-            def _():
-                z_up().start()
-
-            @pl.when(d > 0)
-            def _():
-                z_down().start()
-
         @pl.when(t < nt - 1)
         def _():
             x_up(k).start()
@@ -187,8 +178,13 @@
         def _():
             x_down(k).start()
 
-    for copy in mats:
-        copy.wait()
+        @pl.when(d < nd - 1)
+        def _():
+            z_copy(k, True).start()
+
+        @pl.when(d > 0)
+        def _():
+            z_copy(k, False).start()
 
     def before_halo(k, _):
         lane = pl.multiple_of(chunk(k) * LC, LC)
@@ -212,14 +208,6 @@
 
     lax.fori_loop(0, nc, before_halo, 0)
 
-    @pl.when(d > 0)
-    def _():
-        z_up().wait_recv()
-
-    @pl.when(d < nd - 1)
-    def _():
-        z_down().wait_recv()
-
     low = lax.broadcasted_iota(jnp.int32, (cx, 128), 1) < OW
 
     def send(owner):
@@ -236,31 +224,54 @@
             device_id=(d, t), device_id_type=MESH,
         )
 
+    def wait_halo(k):
+        @pl.when(t > 0)
+        def _():
+            x_up(k).wait_recv()
+
+        @pl.when(t < nt - 1)
+        def _():
+            x_down(k).wait_recv()
+
+        @pl.when(d > 0)
+        def _():
+            z_arrival(k, True).wait_recv()
+
+        @pl.when(d < nd - 1)
+        def _():
+            z_arrival(k, False).wait_recv()
+
+    def stencil(k, z0):
+        lane = pl.multiple_of(chunk(k) * LC, LC)
+        slab = jnp.concatenate(
+            [
+                vp[z0 : z0 + ZB + 4, :, pl.ds(pl.multiple_of(lane + PAD, PAD), LC)].reshape((ZB + 4) * cx, LC),
+                xhl[z0 * 2 : (z0 + ZB) * 2, pl.ds(lane, LC)],
+                xhr[z0 * 2 : (z0 + ZB) * 2, pl.ds(lane, LC)],
+                jnp.zeros((32, LC), jnp.bfloat16),
+            ],
+            axis=0,
+        )
+        return jnp.dot(dzx[...], slab, preferred_element_type=jnp.float32)
+
+    wait_halo(0)
+    gbuf[...] = stencil(0, 0)
+
     def after_halo(k, _):
-        @pl.when(t > 0)
-        def _():
-            x_up(k).wait_recv()
-
-        @pl.when(t < nt - 1)
-        def _():
-            x_down(k).wait_recv()
-
-        lane = pl.multiple_of(chunk(k) * LC, LC)
-        inner = pl.multiple_of(lane + PAD, PAD)
+        inner = pl.multiple_of(chunk(k) * LC + PAD, PAD)
         m0 = jnp.zeros((cx, LC), jnp.float32)
         m1 = m0
         m2 = m0
+        g = gbuf
+        after = jnp.minimum(k + 1, nc - 1)
         for z0 in range(0, nz, ZB):
-            slab = jnp.concatenate(
-                [
-                    vp[z0 : z0 + ZB + 4, :, pl.ds(inner, LC)].reshape((ZB + 4) * cx, LC),
-                    xhl[z0 * 2 : (z0 + ZB) * 2, pl.ds(lane, LC)],
-                    xhr[z0 * 2 : (z0 + ZB) * 2, pl.ds(lane, LC)],
-                    jnp.zeros((32, LC), jnp.bfloat16),
-                ],
-                axis=0,
-            )
-            g = jnp.dot(dzx[...], slab, preferred_element_type=jnp.float32)
+            if z0 == nz // 2:
+
+                @pl.when(k < nc - 1)
+                def _():
+                    wait_halo(after)
+
+            ahead = stencil(k, z0 + ZB) if z0 + ZB < nz else stencil(after, 0)
             for j in range(ZB):
                 here = slice((z0 + j) * cx, (z0 + j + 1) * cx)
                 p = g[j * cx : (j + 1) * cx]
@@ -273,6 +284,8 @@
                 m0 = m0 + w
                 m1 = m1 + wf
                 m2 = m2 + wf * f
+            g = ahead
+        gbuf[...] = g
         s = ss[k]
         for q in range(per):
             part = slice((q // 2) * 128, (q // 2 + 1) * 128)
@@ -330,14 +343,6 @@
     o_ref[2] = (a + 0.25 * b - 0.1 * c)[:, :OW]
     o_ref[3] = (1.0 - jnp.exp2(-ahead))[:, :OW]
 
-    @pl.when(d < nd - 1)
-    def _():
-        z_up().wait_send()
-
-    @pl.when(d > 0)
-    def _():
-        z_down().wait_send()
-
     for k in range(nc):
 
         @pl.when(t < nt - 1)
@@ -347,6 +352,14 @@
         @pl.when(t > 0)
         def _():
             x_down(k).wait_send()
+
+        @pl.when(d < nd - 1)
+        def _():
+            z_copy(k, True).wait_send()
+
+        @pl.when(d > 0)
+        def _():
+            z_copy(k, False).wait_send()
 
     for i in range(nd):
 
@@ -365,7 +378,7 @@
         return pl.pallas_call(
             functools.partial(kernel, nd, nt),
             out_shape=jax.ShapeDtypeStruct((4, cx, OW), jnp.float32),
-            in_specs=[pl.BlockSpec(memory_space=pl.ANY)] * 3,
+            in_specs=[pl.BlockSpec(memory_space=pl.ANY)],
             out_specs=pl.BlockSpec(memory_space=pltpu.VMEM),
             scratch_shapes=[
                 pltpu.VMEM((nz + 4, cx, ny + 2 * PAD), jnp.bfloat16),
@@ -382,10 +395,10 @@
                 pltpu.VMEM((nd, 2, cx, 128), jnp.bfloat16),
                 pltpu.VMEM((nd, 2, cx, 128), jnp.bfloat16),
                 pltpu.VMEM((nd, 2, cx, 128), jnp.float32),
+                pltpu.VMEM((256, LC), jnp.float32),
                 pltpu.SemaphoreType.DMA((nc,)),
-                pltpu.SemaphoreType.DMA((2,)),
-                pltpu.SemaphoreType.DMA((2,)),
-                pltpu.SemaphoreType.DMA((2,)),
+                pltpu.SemaphoreType.DMA((2, nc)),
+                pltpu.SemaphoreType.DMA((2, nc)),
                 pltpu.SemaphoreType.DMA((2, nc)),
                 pltpu.SemaphoreType.DMA((2, nc)),
                 pltpu.SemaphoreType.DMA((nd,)),
@@ -394,7 +407,7 @@
             compiler_params=pltpu.CompilerParams(
                 collective_id=0, has_side_effects=True, vmem_limit_bytes=60 * 2**20
             ),
-        )(volume, jnp.asarray(stencil_zx()), jnp.asarray(stencil_y()))
+        )(volume)
 
     return jax.shard_map(
         body,

time: 22.5 us -> 22.3 us (level)
  no operation moved by 1% of the time
where the time goes in v4:
time: 22.3 us; the launch traced here: 22.1 us
  Pallas kernels  20.7 us (93%)
  local copies, waits for them, and re-layouts  1.38 us (6%)
    pallas_call x1, Pallas kernels, body(): pl.pallas_call(functools.partial(kernel, nd, nt), out_shape=jax.ShapeDtyp...  20.7 us
    unnamed x1, local copies, waits for them, and re-layouts  1.38 us

profile of v4, /device:TPU:2, one launch (start us, length us, event | category | flops | bytes accessed | tf_op | source)
XLA Modules:
  0.0 22.1 jit_solution(8768367721875144408)
XLA Ops:
  0.0 20.7 %shard_map.17 = f32[4,16,64]{2,1,0:T(8,128)} custom-call(bf16[64,16,1024]{2,1,0:T(8,128)(2,1)} %v_ref.1), custom_call_target="tpu_custom_call" | custom-call | tf_op jit(solution)/shard_map/pallas_call | solution.py:378
  20.7 1.4 %copy.3 = f32[4,16,64]{2,1,0:T(8,128)} copy(f32[4,16,64]{2,1,0:T(8,128)} %shard_map.17) | data formatting | bytes 32768

commit v5 on v4

--- a/solution.py
+++ b/solution.py
@@ -264,13 +264,12 @@
         m2 = m0
         g = gbuf
         after = jnp.minimum(k + 1, nc - 1)
+
+        @pl.when(k < nc - 1)
+        def _():
+            wait_halo(after)
+
         for z0 in range(0, nz, ZB):
-            if z0 == nz // 2:
-
-                @pl.when(k < nc - 1)
-                def _():
-                    wait_halo(after)
-
             ahead = stencil(k, z0 + ZB) if z0 + ZB < nz else stencil(after, 0)
             for j in range(ZB):
                 here = slice((z0 + j) * cx, (z0 + j + 1) * cx)
@@ -405,7 +404,7 @@
                 pltpu.SemaphoreType.DMA((nd,)),
             ],
             compiler_params=pltpu.CompilerParams(
-                collective_id=0, has_side_effects=True, vmem_limit_bytes=60 * 2**20
+                collective_id=0, has_side_effects=True, vmem_limit_bytes=105 * 2**19
             ),
         )(volume)
 

time: 22.3 us -> 20.4 us (0.915)
  the two profiles are of different devices: /device:TPU:2 before, /device:TPU:1 now
where the time goes in v5:
time: 20.4 us; the launch traced here: 20.3 us
  Pallas kernels  19.7 us (97%)
  local copies, waits for them, and re-layouts  0.62 us (3%)
    pallas_call x1, Pallas kernels, body(): pl.pallas_call(functools.partial(kernel, nd, nt), out_shape=jax.ShapeDtyp...  19.7 us
    unnamed x1, local copies, waits for them, and re-layouts  0.62 us

profile of v5, /device:TPU:1, one launch (start us, length us, event | category | flops | bytes accessed | tf_op | source)
XLA Modules:
  0.0 20.3 jit_solution(11807886252987880547)
XLA Ops:
  0.0 19.7 %shard_map.17 = f32[4,16,64]{2,1,0:T(8,128)S(1)} custom-call(bf16[64,16,1024]{2,1,0:T(8,128)(2,1)} %v_ref.1), custom_call_target="tpu_custom_call" | custom-call | tf_op jit(solution)/shard_map/pallas_call | solution.py:377
  19.7 0.6 %copy.3 = f32[4,16,64]{2,1,0:T(8,128)} copy(f32[4,16,64]{2,1,0:T(8,128)S(1)} %shard_map.17) | data formatting | bytes 32768

commit v6 on v5

--- a/solution.py
+++ b/solution.py
@@ -52,8 +52,8 @@
     return jnp.where(u < 0.0, -size, size)
 
 
-def kernel(nd, nt, v_ref, o_ref, vp, xhl, xhr, elo, ehi, gy2, gyq, wt, ss, dzx, dy,
-           sb, rb, got, gbuf, load_sem, zs, zr, xs, xr, cs, cr):
+def kernel(nd, nt, v_ref, o_ref, vp, xhl, xhr, elo, ehi, gy2, gyq, wt, wt1, wt2, ss, dzx, dy,
+           sb, rb, got, load_sem, zs, zr, xs, xr, cs, cr, ready):
     nz, cx, ny = v_ref.shape
     nc = ny // LC
     per = LC // OW
@@ -94,8 +94,21 @@
     def _():
         greet(d, t + 1)
 
-    for i in (1, nd - 1, *range(2, nd - 1)):
-        greet(lax.rem(d + i, nd), t)
+    crosses_up = (col == per - 1) & (d < nd - 1)
+    crosses_down = (col == 0) & (d > 0)
+
+    @pl.when(crosses_up)
+    def _():
+        greet(d + 1, t)
+
+    @pl.when(crosses_down)
+    def _():
+        greet(d - 1, t)
+
+    for i in range(1, per):
+        greet(row * per + lax.rem(col + i, per), t)
+    for i in range(1, nc):
+        greet(lax.rem(row + i, nc) * per + col, t)
 
     zeros = jnp.zeros((nz, cx, PAD), jnp.bfloat16)
     vp[2 : 2 + nz, :, 0:PAD] = zeros
@@ -145,17 +158,15 @@
         )
 
     def x_up(k):
-        lane = pl.ds(pl.multiple_of(chunk(k) * LC, LC), LC)
-        return pltpu.make_async_remote_copy(
-            src_ref=ehi.at[:, lane], dst_ref=xhl.at[:, lane],
+        return pltpu.make_async_remote_copy(
+            src_ref=ehi.at[k], dst_ref=xhl.at[k],
             send_sem=xs.at[0, k], recv_sem=xr.at[0, k],
             device_id=(d, lax.rem(t + 1, nt)), device_id_type=MESH,
         )
 
     def x_down(k):
-        lane = pl.ds(pl.multiple_of(chunk(k) * LC, LC), LC)
-        return pltpu.make_async_remote_copy(
-            src_ref=elo.at[:, lane], dst_ref=xhr.at[:, lane],
+        return pltpu.make_async_remote_copy(
+            src_ref=elo.at[k], dst_ref=xhr.at[k],
             send_sem=xs.at[1, k], recv_sem=xr.at[1, k],
             device_id=(d, lax.rem(t + nt - 1, nt)), device_id_type=MESH,
         )
@@ -164,10 +175,12 @@
         load(k).wait()
         lane = pl.multiple_of(chunk(k) * LC, LC)
         rows = vp[2 : 2 + nz, :, pl.ds(pl.multiple_of(lane + PAD, PAD), LC)]
-        elo[:, pl.ds(lane, LC)] = rows[:, 0:2].reshape(nz * 2, LC)
-        ehi[:, pl.ds(lane, LC)] = rows[:, cx - 2 : cx].reshape(nz * 2, LC)
+        elo[k] = rows[:, 0:2].reshape(nz * 2, LC)
+        ehi[k] = rows[:, cx - 2 : cx].reshape(nz * 2, LC)
         if k == 0:
-            waits = nd - 1 + (t > 0).astype(jnp.int32) + (t < nt - 1).astype(jnp.int32)
+            waits = per - 1 + nc - 1
+            for there in (t > 0, t < nt - 1, crosses_up, crosses_down):
+                waits = waits + there.astype(jnp.int32)
             pl.semaphore_wait(barrier, waits)
 
         @pl.when(t < nt - 1)
@@ -185,11 +198,18 @@
         @pl.when(d > 0)
         def _():
             z_copy(k, False).start()
+
+    for i in range(1, nc):
+        pl.semaphore_signal(
+            ready, inc=1, device_id=(lax.rem(row + i, nc) * per + col, t), device_id_type=MESH
+        )
 
     def before_halo(k, _):
         lane = pl.multiple_of(chunk(k) * LC, LC)
         total = jnp.zeros((cx, LC), jnp.float32)
         last = jnp.ones((cx, LC), jnp.float32)
+        sum1 = total
+        sum2 = total
         part = min(256 // cx, nz)
         for z0 in range(0, nz, part):
             slab = vp[2 + z0 : 2 + z0 + part, :, pl.ds(lane, LC + 2 * PAD)]
@@ -199,14 +219,27 @@
             gyq[k, z0 * cx : (z0 + part) * cx] = g * g * 1.25 + 720.0
             for z in range(z0, z0 + part):
                 f = vp[2 + z, :, pl.ds(pl.multiple_of(lane + PAD, PAD), LC)].astype(jnp.float32)
-                total = total + f * f
+                ff = f * f
+                total = total + ff
                 now = jnp.exp2(total * -scale - scale * (z + 1))
-                wt[k, z * cx : (z + 1) * cx] = last - now
+                w = last - now
+                wf = w * f
+                wff = w * ff
+                here = slice(z * cx, (z + 1) * cx)
+                wt[k, here] = w
+                wt1[k, here] = wf
+                wt2[k, here] = wff
+                sum1 = sum1 + wf
+                sum2 = sum2 + wff
                 last = now
-        ss[k] = total * scale + scale * nz
+        ss[k, 0] = BASE * (1.0 - last)
+        ss[k, 1] = BASE * sum1
+        ss[k, 2] = BASE * sum2
+        ss[k, 3] = total * scale + scale * nz
         return 0
 
     lax.fori_loop(0, nc, before_halo, 0)
+    pl.semaphore_wait(ready, nc - 1)
 
     low = lax.broadcasted_iota(jnp.int32, (cx, 128), 1) < OW
 
@@ -246,46 +279,29 @@
         slab = jnp.concatenate(
             [
                 vp[z0 : z0 + ZB + 4, :, pl.ds(pl.multiple_of(lane + PAD, PAD), LC)].reshape((ZB + 4) * cx, LC),
-                xhl[z0 * 2 : (z0 + ZB) * 2, pl.ds(lane, LC)],
-                xhr[z0 * 2 : (z0 + ZB) * 2, pl.ds(lane, LC)],
+                xhl[k, z0 * 2 : (z0 + ZB) * 2],
+                xhr[k, z0 * 2 : (z0 + ZB) * 2],
                 jnp.zeros((32, LC), jnp.bfloat16),
             ],
             axis=0,
         )
         return jnp.dot(dzx[...], slab, preferred_element_type=jnp.float32)
 
-    wait_halo(0)
-    gbuf[...] = stencil(0, 0)
-
     def after_halo(k, _):
-        inner = pl.multiple_of(chunk(k) * LC + PAD, PAD)
-        m0 = jnp.zeros((cx, LC), jnp.float32)
-        m1 = m0
-        m2 = m0
-        g = gbuf
-        after = jnp.minimum(k + 1, nc - 1)
-
-        @pl.when(k < nc - 1)
-        def _():
-            wait_halo(after)
-
+        m0, m1, m2 = ss[k, 0], ss[k, 1], ss[k, 2]
+        wait_halo(k)
         for z0 in range(0, nz, ZB):
-            ahead = stencil(k, z0 + ZB) if z0 + ZB < nz else stencil(after, 0)
+            g = stencil(k, z0)
             for j in range(ZB):
                 here = slice((z0 + j) * cx, (z0 + j + 1) * cx)
                 p = g[j * cx : (j + 1) * cx]
                 q = g[128 + j * cx : 128 + (j + 1) * cx]
                 facing = jnp.abs(p + gy2[k, here])
                 facing = facing * lax.rsqrt(p * p + q * q + gyq[k, here])
-                w = wt[k, here] * (facing + BASE)
-                f = vp[2 + z0 + j, :, pl.ds(inner, LC)].astype(jnp.float32)
-                wf = w * f
-                m0 = m0 + w
-                m1 = m1 + wf
-                m2 = m2 + wf * f
-            g = ahead
-        gbuf[...] = g
-        s = ss[k]
+                m0 = m0 + facing * wt[k, here]
+                m1 = m1 + facing * wt1[k, here]
+                m2 = m2 + facing * wt2[k, here]
+        s = ss[k, 3]
         for q in range(per):
             part = slice((q // 2) * 128, (q // 2 + 1) * 128)
             a, b, c, e = m0[:, part], m1[:, part], m2[:, part], s[:, part]
@@ -324,7 +340,32 @@
             take(lax.rem(row + n, nc), q)
         return 0
 
-    lax.fori_loop(1, nc + 1, other_row, 0)
+    lax.fori_loop(1, nc, other_row, 0)
+    for k in range(nc):
+
+        @pl.when(t < nt - 1)
+        def _():
+            x_up(k).wait_send()
+
+        @pl.when(t > 0)
+        def _():
+            x_down(k).wait_send()
+
+        @pl.when(d < nd - 1)
+        def _():
+            z_copy(k, True).wait_send()
+
+        @pl.when(d > 0)
+        def _():
+            z_copy(k, False).wait_send()
+
+    for i in range(nd):
+
+        @pl.when(d != i)
+        def _():
+            send(i).wait_send()
+    for q in range(per):
+        take(row, q)
     ahead = jnp.zeros((cx, 128), jnp.float32)
     acc0 = ahead
     acc1 = ahead
@@ -342,30 +383,6 @@
     o_ref[2] = (a + 0.25 * b - 0.1 * c)[:, :OW]
     o_ref[3] = (1.0 - jnp.exp2(-ahead))[:, :OW]
 
-    for k in range(nc):
-
-        @pl.when(t < nt - 1)
-        def _():
-            x_up(k).wait_send()
-
-        @pl.when(t > 0)
-        def _():
-            x_down(k).wait_send()
-
-        @pl.when(d < nd - 1)
-        def _():
-            z_copy(k, True).wait_send()
-
-        @pl.when(d > 0)
-        def _():
-            z_copy(k, False).wait_send()
-
-    for i in range(nd):
-
-        @pl.when(d != i)
-        def _():
-            send(i).wait_send()
-
 
 def solution(mesh):
     nd, nt = mesh.shape["depth"], mesh.shape["tile"]
@@ -381,20 +398,21 @@
             out_specs=pl.BlockSpec(memory_space=pltpu.VMEM),
             scratch_shapes=[
                 pltpu.VMEM((nz + 4, cx, ny + 2 * PAD), jnp.bfloat16),
-                pltpu.VMEM((nz * 2, ny), jnp.bfloat16),
-                pltpu.VMEM((nz * 2, ny), jnp.bfloat16),
-                pltpu.VMEM((nz * 2, ny), jnp.bfloat16),
-                pltpu.VMEM((nz * 2, ny), jnp.bfloat16),
+                pltpu.VMEM((nc, nz * 2, LC), jnp.bfloat16),
+                pltpu.VMEM((nc, nz * 2, LC), jnp.bfloat16),
+                pltpu.VMEM((nc, nz * 2, LC), jnp.bfloat16),
+                pltpu.VMEM((nc, nz * 2, LC), jnp.bfloat16),
                 pltpu.VMEM(big, jnp.float32),
                 pltpu.VMEM(big, jnp.float32),
                 pltpu.VMEM(big, jnp.float32),
-                pltpu.VMEM((nc, cx, LC), jnp.float32),
+                pltpu.VMEM(big, jnp.float32),
+                pltpu.VMEM(big, jnp.float32),
+                pltpu.VMEM((nc, 4, cx, LC), jnp.float32),
                 pltpu.VMEM((256, 256), jnp.bfloat16),
                 pltpu.VMEM((LC + 2 * PAD, LC), jnp.bfloat16),
                 pltpu.VMEM((nd, 2, cx, 128), jnp.bfloat16),
                 pltpu.VMEM((nd, 2, cx, 128), jnp.bfloat16),
                 pltpu.VMEM((nd, 2, cx, 128), jnp.float32),
-                pltpu.VMEM((256, LC), jnp.float32),
                 pltpu.SemaphoreType.DMA((nc,)),
                 pltpu.SemaphoreType.DMA((2, nc)),
                 pltpu.SemaphoreType.DMA((2, nc)),
@@ -402,6 +420,7 @@
                 pltpu.SemaphoreType.DMA((2, nc)),
                 pltpu.SemaphoreType.DMA((nd,)),
                 pltpu.SemaphoreType.DMA((nd,)),
+                pltpu.SemaphoreType.REGULAR,
             ],
             compiler_params=pltpu.CompilerParams(
                 collective_id=0, has_side_effects=True, vmem_limit_bytes=105 * 2**19

time: 20.4 us -> 20.1 us (0.985)
  the two profiles are of different devices: /device:TPU:1 before, /device:TPU:2 now
where the time goes in v6:
time: 20.1 us; the launch traced here: 19.9 us
  Pallas kernels  19.3 us (96%)
  local copies, waits for them, and re-layouts  0.62 us (3%)
    pallas_call x1, Pallas kernels, body(): pl.pallas_call(functools.partial(kernel, nd, nt), out_shape=jax.ShapeDtyp...  19.3 us
    unnamed x1, local copies, waits for them, and re-layouts  0.62 us

profile of v6, /device:TPU:2, one launch (start us, length us, event | category | flops | bytes accessed | tf_op | source)
XLA Modules:
  0.0 19.9 jit_solution(4158617179710761160)
XLA Ops:
  0.0 19.3 %shard_map.17 = f32[4,16,64]{2,1,0:T(8,128)S(1)} custom-call(bf16[64,16,1024]{2,1,0:T(8,128)(2,1)} %v_ref.1), custom_call_target="tpu_custom_call" | custom-call | tf_op jit(solution)/shard_map/pallas_call | solution.py:394
  19.3 0.6 %copy.3 = f32[4,16,64]{2,1,0:T(8,128)} copy(f32[4,16,64]{2,1,0:T(8,128)S(1)} %shard_map.17) | data formatting | bytes 32768

commit v7 on v6

--- a/solution.py
+++ b/solution.py
@@ -62,6 +62,33 @@
     row, col = d // per, lax.rem(d, per)
     scale = math.log2(math.e) / (nz * nd)
 
+    barrier = pltpu.get_barrier_semaphore()
+
+    def greet(depth, tile):
+        pl.semaphore_signal(barrier, inc=1, device_id=(depth, tile), device_id_type=MESH)
+
+    for i in range(1, per):
+        greet(row * per + lax.rem(col + i, per), t)
+
+    @pl.when(t > 0)
+    def _():
+        greet(d, t - 1)
+
+    @pl.when(t < nt - 1)
+    def _():
+        greet(d, t + 1)
+
+    crosses_up = (col == per - 1) & (d < nd - 1)
+    crosses_down = (col == 0) & (d > 0)
+
+    @pl.when(crosses_up)
+    def _():
+        greet(d + 1, t)
+
+    @pl.when(crosses_down)
+    def _():
+        greet(d - 1, t)
+
     def chunk(k, r=None):
         r = row if r is None else r
         if nc != 4:
@@ -81,32 +108,6 @@
     for k in range(nc):
         load(k).start()
 
-    barrier = pltpu.get_barrier_semaphore()
-
-    def greet(depth, tile):
-        pl.semaphore_signal(barrier, inc=1, device_id=(depth, tile), device_id_type=MESH)
-
-    @pl.when(t > 0)
-    def _():
-        greet(d, t - 1)
-
-    @pl.when(t < nt - 1)
-    def _():
-        greet(d, t + 1)
-
-    crosses_up = (col == per - 1) & (d < nd - 1)
-    crosses_down = (col == 0) & (d > 0)
-
-    @pl.when(crosses_up)
-    def _():
-        greet(d + 1, t)
-
-    @pl.when(crosses_down)
-    def _():
-        greet(d - 1, t)
-
-    for i in range(1, per):
-        greet(row * per + lax.rem(col + i, per), t)
     for i in range(1, nc):
         greet(lax.rem(row + i, nc) * per + col, t)
 
@@ -138,12 +139,17 @@
     for i in range(0, LC + 2 * PAD, PAD):
         dy[i : i + PAD] = (2.0 * taps(src - dst + (i - PAD))).astype(jnp.bfloat16)
 
-    def z_copy(k, up):
+    def z_copy(k, up, across):
         there = lax.rem(d + (1 if up else nd - 1), nd)
         lane = pl.multiple_of(chunk(k, there // per) * LC, LC)
-        return pltpu.make_async_remote_copy(
-            src_ref=v_ref.at[pl.ds(nz - 2 if up else 0, 2), :, pl.ds(lane, LC)],
-            dst_ref=vp.at[pl.ds(0 if up else nz + 2, 2), :, pl.ds(pl.multiple_of(lane + PAD, PAD), LC)],
+        inner = pl.ds(pl.multiple_of(lane + PAD, PAD), LC)
+        if across:
+            src = v_ref.at[pl.ds(nz - 2 if up else 0, 2), :, pl.ds(lane, LC)]
+        else:
+            src = vp.at[pl.ds(nz if up else 2, 2), :, inner]
+        return pltpu.make_async_remote_copy(
+            src_ref=src,
+            dst_ref=vp.at[pl.ds(0 if up else nz + 2, 2), :, inner],
             send_sem=zs.at[1 - up, k], recv_sem=zr.at[1 - up, k],
             device_id=(there, t), device_id_type=MESH,
         )
@@ -183,6 +189,22 @@
                 waits = waits + there.astype(jnp.int32)
             pl.semaphore_wait(barrier, waits)
 
+        @pl.when(col < per - 1)
+        def _():
+            z_copy(k, True, False).start()
+
+        @pl.when(col > 0)
+        def _():
+            z_copy(k, False, False).start()
+
+        @pl.when(crosses_up)
+        def _():
+            z_copy(k, True, True).start()
+
+        @pl.when(crosses_down)
+        def _():
+            z_copy(k, False, True).start()
+
         @pl.when(t < nt - 1)
         def _():
             x_up(k).start()
@@ -190,14 +212,6 @@
         @pl.when(t > 0)
         def _():
             x_down(k).start()
-
-        @pl.when(d < nd - 1)
-        def _():
-            z_copy(k, True).start()
-
-        @pl.when(d > 0)
-        def _():
-            z_copy(k, False).start()
 
     for i in range(1, nc):
         pl.semaphore_signal(
@@ -353,11 +367,11 @@
 
         @pl.when(d < nd - 1)
         def _():
-            z_copy(k, True).wait_send()
+            z_copy(k, True, False).wait_send()
 
         @pl.when(d > 0)
         def _():
-            z_copy(k, False).wait_send()
+            z_copy(k, False, False).wait_send()
 
     for i in range(nd):
 

time: 20.1 us -> 20.1 us (level)
  no operation moved by 1% of the time
where the time goes in v7:
time: 20.1 us; the launch traced here: 20 us
  Pallas kernels  19.3 us (96%)
  local copies, waits for them, and re-layouts  0.62 us (3%)
    pallas_call x1, Pallas kernels, body(): pl.pallas_call(functools.partial(kernel, nd, nt), out_shape=jax.ShapeDtyp...  19.3 us
    unnamed x1, local copies, waits for them, and re-layouts  0.62 us

profile of v7, /device:TPU:2, one launch (start us, length us, event | category | flops | bytes accessed | tf_op | source)
XLA Modules:
  0.0 20.0 jit_solution(3048035205831743414)
XLA Ops:
  0.0 19.3 %shard_map.17 = f32[4,16,64]{2,1,0:T(8,128)S(1)} custom-call(bf16[64,16,1024]{2,1,0:T(8,128)(2,1)} %v_ref.1), custom_call_target="tpu_custom_call" | custom-call | tf_op jit(solution)/shard_map/pallas_call | solution.py:408
  19.3 0.6 %copy.3 = f32[4,16,64]{2,1,0:T(8,128)} copy(f32[4,16,64]{2,1,0:T(8,128)S(1)} %shard_map.17) | data formatting | bytes 32768

commit v8 on v7

--- a/solution.py
+++ b/solution.py
@@ -139,14 +139,11 @@
     for i in range(0, LC + 2 * PAD, PAD):
         dy[i : i + PAD] = (2.0 * taps(src - dst + (i - PAD))).astype(jnp.bfloat16)
 
-    def z_copy(k, up, across):
+    def z_copy(k, up):
         there = lax.rem(d + (1 if up else nd - 1), nd)
         lane = pl.multiple_of(chunk(k, there // per) * LC, LC)
         inner = pl.ds(pl.multiple_of(lane + PAD, PAD), LC)
-        if across:
-            src = v_ref.at[pl.ds(nz - 2 if up else 0, 2), :, pl.ds(lane, LC)]
-        else:
-            src = vp.at[pl.ds(nz if up else 2, 2), :, inner]
+        src = vp.at[pl.ds(nz if up else 2, 2), :, inner]
         return pltpu.make_async_remote_copy(
             src_ref=src,
             dst_ref=vp.at[pl.ds(0 if up else nz + 2, 2), :, inner],
@@ -177,8 +174,22 @@
             device_id=(d, lax.rem(t + nt - 1, nt)), device_id_type=MESH,
         )
 
+    crosses = crosses_up | crosses_down
     for k in range(nc):
-        load(k).wait()
+        if k == 0:
+            load(0).wait()
+
+            @pl.when(crosses)
+            def _():
+                for later in range(1, nc):
+                    load(later).wait()
+
+        else:
+
+            @pl.when(jnp.logical_not(crosses))
+            def _():
+                load(k).wait()
+
         lane = pl.multiple_of(chunk(k) * LC, LC)
         rows = vp[2 : 2 + nz, :, pl.ds(pl.multiple_of(lane + PAD, PAD), LC)]
         elo[k] = rows[:, 0:2].reshape(nz * 2, LC)
@@ -189,21 +200,13 @@
                 waits = waits + there.astype(jnp.int32)
             pl.semaphore_wait(barrier, waits)
 
-        @pl.when(col < per - 1)
-        def _():
-            z_copy(k, True, False).start()
-
-        @pl.when(col > 0)
-        def _():
-            z_copy(k, False, False).start()
-
-        @pl.when(crosses_up)
-        def _():
-            z_copy(k, True, True).start()
-
-        @pl.when(crosses_down)
-        def _():
-            z_copy(k, False, True).start()
+        @pl.when(d < nd - 1)
+        def _():
+            z_copy(k, True).start()
+
+        @pl.when(d > 0)
+        def _():
+            z_copy(k, False).start()
 
         @pl.when(t < nt - 1)
         def _():
@@ -367,11 +370,11 @@
 
         @pl.when(d < nd - 1)
         def _():
-            z_copy(k, True, False).wait_send()
+            z_copy(k, True).wait_send()
 
         @pl.when(d > 0)
         def _():
-            z_copy(k, False, False).wait_send()
+            z_copy(k, False).wait_send()
 
     for i in range(nd):
 

time: 20.1 us -> 19.9 us (0.990)
    pallas_call x1, Pallas kernels: 19.3 us -> 19.1 us  [body(): pl.pallas_call(functools.partial(kernel, nd, nt), out_shape=jax.ShapeDtyp...]
where the time goes in v8:
time: 19.9 us; the launch traced here: 19.7 us
  Pallas kernels  19.1 us (96%)
  local copies, waits for them, and re-layouts  0.62 us (3%)
    pallas_call x1, Pallas kernels, body(): pl.pallas_call(functools.partial(kernel, nd, nt), out_shape=jax.ShapeDtyp...  19.1 us
    unnamed x1, local copies, waits for them, and re-layouts  0.62 us

profile of v8, /device:TPU:2, one launch (start us, length us, event | category | flops | bytes accessed | tf_op | source)
XLA Modules:
  0.0 19.7 jit_solution(17639143916152623342)
XLA Ops:
  0.0 19.1 %shard_map.17 = f32[4,16,64]{2,1,0:T(8,128)S(1)} custom-call(bf16[64,16,1024]{2,1,0:T(8,128)(2,1)} %v_ref.1), custom_call_target="tpu_custom_call" | custom-call | tf_op jit(solution)/shard_map/pallas_call | solution.py:411
  19.1 0.6 %copy.3 = f32[4,16,64]{2,1,0:T(8,128)} copy(f32[4,16,64]{2,1,0:T(8,128)S(1)} %shard_map.17) | data formatting | bytes 32768
